TPU v7x, 32 devices: a whole 2x2x4 slice. The times are simulated.
32 devices in a mesh: mesh: 8 (over z, x), lev: 4 (over y, core).
Axes of the slice: x: 2, y: 2, z: 4, core: 2. Of those that a mesh axis runs over, the one named last changes fastest.
Arguments:
- velocity: float32 [8, 24576], P('lev', 'mesh'), may hold values from -6 to 6
- thickness: float32 [8, 24576], P('lev', 'mesh'), may hold values from 0.5 to 2
- vorticity: float32 [8, 24576], P('lev', 'mesh'), may hold values from -6 to 6
- vertical_wind: float32 [8, 24576], P('lev', 'mesh'), may hold values from -6 to 6
- weights_on_edge: float32 [10, 24576], P(None, 'mesh'), may hold values from -2 to 2
- edges_on_edge: int32 [10, 24576], P(None, 'mesh'), may hold values from 0 to 3839, as said below
- edges_on_cell: int32 [6, 8192], P(None, 'mesh'), may hold values from 0 to 3839, as said below
- cells_on_edge: int32 [2, 24576], P(None, 'mesh'), may hold values from 0 to 1407, as said below
- energy_weight: float32 [6, 8192], P(None, 'mesh'), may hold values from 0.05 to 0.5
- inverse_distance: float32 [24576], P('mesh'), may hold values from 0.5 to 2
- edge_halo_list: int32 [48, 128], P('mesh'), may hold values from 0 to 3071
- edge_halo_count: int32 [48], P('mesh'), may hold values from 1 to 128, as said below
- cell_halo_list: int32 [48, 64], P('mesh'), may hold values from 0 to 1023
- cell_halo_count: int32 [48], P('mesh'), may hold values from 1 to 64, as said below
Outputs:
- tendency: float32 [8, 24576], P('lev', 'mesh')
- tangent: float32 [8, 24576], P('lev', 'mesh')
- energy: float32 [8, 8192], P('lev', 'mesh')
Inputs may be any that keep to these rules, and one draw needn't show every extreme that they name: `edge_halo_count`: row r names how many leading slots of the halo block r are live. `cell_halo_count`: row r names how many leading slots of the halo block r are live. `edges_on_edge`: entries name local edges or live slots of edge halo blocks. `edges_on_cell`: entries name local edges or live slots of edge halo blocks. `cells_on_edge`: entries name local cells or live slots of cell halo blocks.
All inputs are finite; a program needn't handle non-finite values.
Results may differ from a plain program's by a relative error of at most 0.0003.
Values sent between devices are 32-bit elements; how exact they have to be, the bound alone decides.
A program may use at most 128 MiB of HBM per device.

v0:
```python
import jax
import jax.numpy as jnp
from jax import lax
from jax.sharding import PartitionSpec as P

REACH = 3


def from_behind(block, axis, distance):
    devices = range(lax.axis_size(axis))
    route = [((i - distance) % len(devices), i) for i in devices]
    return lax.ppermute(block, axis, route)


def padded(block, sides, width):
    for axis, dim in sides:
        count = lax.axis_size(axis)
        forward = [(i, i + 1) for i in range(count - 1)]
        backward = [(target, source) for source, target in forward]
        low = lax.ppermute(
            lax.slice_in_dim(block, block.shape[dim] - width, None, axis=dim), axis, forward
        )
        high = lax.ppermute(lax.slice_in_dim(block, 0, width, axis=dim), axis, backward)
        block = jnp.concatenate([low, block, high], axis=dim)
    return block


def pack_blocks(fields, halo_list, halo_count):
    breadth = halo_list.shape[1]
    picked = jnp.take(fields, halo_list.reshape(-1), axis=2)
    picked = picked.reshape(fields.shape[0], fields.shape[1], halo_list.shape[0], breadth)
    living = jnp.arange(breadth)[None, :] < halo_count[:, None]
    return jnp.where(living[None, None], picked, 0.0)


def route_edges(blocks):
    pieces = []
    for block_index in range(2 * REACH):
        offset = block_index + 1 if block_index < REACH else REACH - 1 - block_index
        pieces.append(from_behind(blocks[:, :, block_index, :], "mesh", offset))
    return jnp.stack(pieces, axis=2)


def route_cells(blocks):
    pieces = []
    for block_index in range(2 * REACH):
        offset = block_index + 1 if block_index < REACH else REACH - 1 - block_index
        pieces.append(from_behind(blocks[:, :, block_index, :], "mesh", offset))
    return jnp.stack(pieces, axis=2)


def lookup(field, table):
    return jnp.take(field, table.reshape(-1), axis=1).reshape(
        field.shape[0], table.shape[0], table.shape[1]
    )


def body(
    velocity,
    thickness,
    vorticity,
    vertical_wind,
    weights_on_edge,
    edges_on_edge,
    edges_on_cell,
    cells_on_edge,
    energy_weight,
    inverse_distance,
    edge_halo_list,
    edge_halo_count,
    cell_halo_list,
    cell_halo_count,
):
    levels, edge_total = velocity.shape
    fields = jnp.stack([velocity, thickness, vorticity])
    received = route_edges(pack_blocks(fields, edge_halo_list, edge_halo_count))
    extended = jnp.concatenate([fields, received.reshape(3, levels, -1)], axis=2)
    speed_near = lookup(extended[0], edges_on_edge)
    tangent = jnp.sum(weights_on_edge * speed_near, axis=1)
    height_near = lookup(extended[1], edges_on_edge)
    moved = weights_on_edge * speed_near * height_near
    potential_near = lookup(extended[2], edges_on_edge)
    flux = jnp.sum(moved * 0.5 * (vorticity[:, None, :] + potential_near), axis=1)
    cell_speed = lookup(extended[0], edges_on_cell)
    energy = jnp.sum(energy_weight * cell_speed * cell_speed, axis=1)
    cell_received = route_cells(pack_blocks(energy[None], cell_halo_list, cell_halo_count))
    cell_extended = jnp.concatenate([energy, cell_received[0].reshape(levels, -1)], axis=1)
    ends = lookup(cell_extended, cells_on_edge)
    gradient = (ends[:, 1] - ends[:, 0]) * inverse_distance
    rims = padded(velocity, (("lev", 0),), 1)
    advect = -0.5 * vertical_wind * (rims[2:] - rims[:-2])
    tendency = flux - gradient + advect
    return (tendency, tangent, energy)


def solution(mesh):
    in_specs = (
        P("lev", "mesh"),
        P("lev", "mesh"),
        P("lev", "mesh"),
        P("lev", "mesh"),
        P(None, "mesh"),
        P(None, "mesh"),
        P(None, "mesh"),
        P(None, "mesh"),
        P(None, "mesh"),
        P("mesh"),
        P("mesh", None),
        P("mesh"),
        P("mesh", None),
        P("mesh"),
    )
    out_specs = (P("lev", "mesh"), P("lev", "mesh"), P("lev", "mesh"))
    return jax.shard_map(body, mesh=mesh, in_specs=in_specs, out_specs=out_specs, check_vma=False)
```

profile of v0, /device:TPU:0, one launch (start us, length us, event | category | flops | bytes accessed | tf_op | source)
XLA Modules:
  0.0 527.8 jit_solution(15284308991441722497)
XLA Ops:
  0.6 1.4 fusion.10
  2.1 1.3 collective-permute-start.12
  3.4 3.6 collective-permute-start.13
  7.0 0.8 reshape.272
  7.8 0.8 iota_compare_fusion.1
  8.5 0.7 fusion.8
  9.3 0.8 pad_maximum_fusion.2
  10.1 2.9 copy.166
  13.0 3.2 gather_fusion
  16.2 1.3 copy.167
  17.6 5.0 collective-permute-start.5
  22.6 1.3 collective-permute-start.4
  23.9 0.6 collective-permute-start
  24.6 0.9 reshape.267
  25.5 0.6 compare_and_fusion
  26.2 0.7 fusion.1
  26.9 1.4 compare_and_fusion.2
  28.2 0.8 compare_and_fusion.1
  29.0 0.8 copy.192
  29.8 0.8 copy.191
  30.6 0.6 broadcast_clamp_fusion
  31.3 1.4 iota_compare_fusion
  32.6 1.2 copy.175
  33.9 1.6 collective-permute-start.1
  35.5 3.8 collective-permute-done.1
  39.3 0.7 collective-permute-start.2
  40.0 4.7 collective-permute-done.2
  44.7 1.4 collective-permute-start.3
  46.1 2.6 collective-permute-done.3
  48.7 0.8 pad_maximum_fusion.1
  49.5 0.6 slice_bitcast_fusion.1
  50.2 1.9 copy.174
  52.1 1.3 copy.173
  53.4 2.6 copy.176
  56.1 22.9 %gather_fusion.1 = f32[6144,2]{1,0:T(8,128)} fusion(f32[2,3840]{0,1:T(8,128)S(1)} %copy.173, s32[6144]{0:T(1024)} %get-tuple-element.54), kind=kCustom, calls=%fused_computation.4 | custom fusion | bytes 122880 | tf_op jit(solution)/shard_map/jit(_take)/gather | solution.py:53
  79.0 5.5 %fusion = f32[2,1024]{0,1:T(8,128)} fusion(f32[2,6,1024]{0,2,1:T(8,128)} %bitcast.116, f32[6,1024]{1,0:T(8,128)} %param.24, pred[6,1024]{1,0:T(8,128)(4,1)} %compare_and_fusion.2), kind=kLoop, calls=%fused_computation.13 | loop fusion | flops 47104 | bytes 88064 | tf_op jit(solution)/shard_map/reduce_sum | solution.py:85
  84.5 1.8 copy.185
  86.3 2.6 gather_fusion.2
  89.0 1.6 copy.178
  90.6 0.7 select_select_fusion.1
  91.3 0.6 slice_bitcast_fusion.9
  91.9 0.3 collective-permute-start.11
  92.2 2.4 collective-permute-start.10
  94.6 1.6 collective-permute-start.6
  96.2 111.4 %gather_fusion.4 = f32[30720,2]{1,0:T(8,128)} fusion(f32[2,3840]{0,1:T(8,128)S(1)} %copy.173, s32[30720]{0:T(1024)} %fusion.1), kind=kCustom, calls=%fused_computation.clone | custom fusion | bytes 614400 | tf_op jit(solution)/shard_map/jit(_take)/gather | solution.py:53
  207.7 113.0 %gather_fusion.6 = f32[30720,2]{1,0:T(8,128)} fusion(f32[2,3840]{0,1:T(8,128)} %copy.176, s32[30720]{0:T(1024)} %fusion.1), kind=kCustom, calls=%fused_computation.2.clone | custom fusion | bytes 614400 | tf_op jit(solution)/shard_map/jit(_take)/gather | solution.py:53
  320.7 113.0 %gather_fusion.5 = f32[30720,2]{1,0:T(8,128)} fusion(f32[2,3840]{0,1:T(8,128)} %copy.174, s32[30720]{0:T(1024)} %fusion.1), kind=kCustom, calls=%fused_computation.1.clone | custom fusion | bytes 614400 | tf_op jit(solution)/shard_map/jit(_take)/gather | solution.py:53
  433.7 32.9 %broadcast_select_fusion.1 = (f32[30720,2]{1,0:T(8,128)}, f32[30720,2]{1,0:T(8,128)}, f32[30720,2]{1,0:T(8,128)}) fusion(f32[30720,2]{1,0:T(8,128)} %gather_fusion.5, pred[30720]{0:T(1024)(128)(4,1)} %compare_and_fusion, f32[30720,2]{1,0:T(8,128)} %gather_fusion.6, f32[30720,2]{1,0:T(8,128)} %gather_fusion.4), kind=kLoop, calls=%fused_computation.10 | loop fusion | flops 184320 | bytes 1505280 | tf_op jit(solution)/shard_map/jit(_take)/select_n | solution.py:53
  466.6 17.2 %multiply_reduce_fusion.1 = (f32[2,3072]{0,1:T(8,128)}, f32[2,3072]{0,1:T(8,128)S(1)}) fusion(f32[2,10,3072]{0,2,1:T(8,128)} %bitcast.115, f32[10,3072]{1,0:T(8,128)S(1)} %copy-done, f32[2,10,3072]{0,2,1:T(8,128)} %bitcast.114, f32[2,3072]{0,1:T(8,128)S(1)} %copy.175, f32[2,10,3072]{0,2,1:T(8,128)} %bitcast.113), kind=kLoop, calls=%fused_computation.8 | loop fusion | flops 417792 | bytes 933888 | tf_op jit(solution)/shard_map/reduce_sum | solution.py:79
  483.8 2.5 copy.184
  486.3 0.5 copy.183
  486.8 0.7 collective-permute-start.7
  487.5 0.6 constant_dynamic-update-slice_fusion.11
  488.2 4.1 collective-permute-done.7
  492.2 1.1 collective-permute-start.8
  493.4 4.2 collective-permute-done.8
  497.6 0.7 collective-permute-start.9
  498.3 3.2 collective-permute-done.9
  501.5 0.7 constant_dynamic-update-slice_fusion.7
  502.2 0.7 constant_dynamic-update-slice_fusion.6
  503.0 2.0 pad_maximum_fusion
  504.9 20.1 %gather_fusion.3 = f32[6144,2]{1,0:T(8,128)S(1)} fusion(f32[2,1408]{0,1:T(8,128)} %pad_maximum_fusion, s32[6144]{0:T(1024)} %get-tuple-element.53), kind=kCustom, calls=%fused_computation.6 | custom fusion | bytes 122880 | tf_op jit(solution)/shard_map/jit(_take)/gather | solution.py:53
  525.1 1.2 copy.182
  526.3 1.5 fusion.4
  (33 shorter events, 0.4 us)
Async XLA Ops:
  2.1 524.2 %collective-permute-start.12 = (f32[1,3072]{1,0:T(1,128)}, f32[1,3072]{1,0:T(1,128)}, u32[]{:S(2)}, u32[]{:S(2)}) collective-permute-start(f32[1,3072]{1,0:T(1,128)} %get-tuple-element.39), channel_id=1, source_target_pairs={{1,0},{2,1},{3,2},{5,4},{6,5},{7,6},{9,8},{10,9},{11,10},{13,12},{... | collective-permute-start | bytes 36872 | tf_op jit(solution)/shard_map/ppermute | solution.py:23
  3.4 523.0 %collective-permute-start.13 = (f32[1,3072]{1,0:T(1,128)}, f32[1,3072]{1,0:T(1,128)}, u32[]{:S(2)}, u32[]{:S(2)}) collective-permute-start(f32[1,3072]{1,0:T(1,128)} %get-tuple-element.40), channel_id=1, source_target_pairs={{0,1},{1,2},{2,3},{4,5},{5,6},{6,7},{8,9},{9,10},{10,11},{12,13},{... | collective-permute-start | bytes 36872 | tf_op jit(solution)/shard_map/ppermute | solution.py:20
  17.6 31.1 %collective-permute-start.5 = (f32[3,2,128]{2,1,0:T(2,128)S(1)}, f32[3,2,128]{2,1,0:T(2,128)S(1)}, u32[]{:S(2)}, u32[]{:S(2)}) collective-permute-start(f32[3,2,128]{2,1,0:T(2,128)S(1)} %get-tuple-element.41), channel_id=1, source_target_pairs={{12,0},{16,4},{20,8},{24,12},{28,16},{0,20},{4,24},{8,28},{13,1},{... | collective-permute-start | bytes 9224 | tf_op jit(solution)/shard_map/ppermute | solution.py:12
  22.6 26.1 %collective-permute-start.4 = (f32[3,2,128]{2,1,0:T(2,128)S(1)}, f32[3,2,128]{2,1,0:T(2,128)S(1)}, u32[]{:S(2)}, u32[]{:S(2)}) collective-permute-start(f32[3,2,128]{2,1,0:T(2,128)S(1)} %get-tuple-element.42), channel_id=1, source_target_pairs={{8,0},{12,4},{16,8},{20,12},{24,16},{28,20},{0,24},{4,28},{9,1},{1... | collective-permute-start | bytes 9224 | tf_op jit(solution)/shard_map/ppermute | solution.py:12
  23.9 9.9 %collective-permute-start = (f32[3,2,128]{2,1,0:T(2,128)S(1)}, f32[3,2,128]{2,1,0:T(2,128)S(1)}, u32[]{:S(2)}, u32[]{:S(2)}) collective-permute-start(f32[3,2,128]{2,1,0:T(2,128)S(1)} %get-tuple-element.46), channel_id=1, source_target_pairs={{28,0},{0,4},{4,8},{8,12},{12,16},{16,20},{20,24},{24,28},{29,1},{... | collective-permute-start | bytes 9224 | tf_op jit(solution)/shard_map/ppermute | solution.py:12
  33.9 5.4 %collective-permute-start.1 = (f32[3,2,128]{2,1,0:T(2,128)S(1)}, f32[3,2,128]{2,1,0:T(2,128)S(1)}, u32[]{:S(2)}, u32[]{:S(2)}) collective-permute-start(f32[3,2,128]{2,1,0:T(2,128)S(1)} %get-tuple-element.45), channel_id=1, source_target_pairs={{24,0},{28,4},{0,8},{4,12},{8,16},{12,20},{16,24},{20,28},{25,1},{... | collective-permute-start | bytes 9224 | tf_op jit(solution)/shard_map/ppermute | solution.py:12
  39.3 5.4 %collective-permute-start.2 = (f32[3,2,128]{2,1,0:T(2,128)S(1)}, f32[3,2,128]{2,1,0:T(2,128)S(1)}, u32[]{:S(2)}, u32[]{:S(2)}) collective-permute-start(f32[3,2,128]{2,1,0:T(2,128)S(1)} %get-tuple-element.44), channel_id=1, source_target_pairs={{20,0},{24,4},{28,8},{0,12},{4,16},{8,20},{12,24},{16,28},{21,1},{... | collective-permute-start | bytes 9224 | tf_op jit(solution)/shard_map/ppermute | solution.py:12
  44.7 4.0 collective-permute-start.3
  91.9 410.3 %collective-permute-start.11 = (f32[1,2,64]{2,1,0:T(2,128)S(1)}, f32[1,2,64]{2,1,0:T(2,128)}, u32[]{:S(2)}, u32[]{:S(2)}) collective-permute-start(f32[1,2,64]{2,1,0:T(2,128)S(1)} %get-tuple-element.47), channel_id=1, source_target_pairs={{12,0},{16,4},{20,8},{24,12},{28,16},{0,20},{4,24},{8,28},{13,1},{... | collective-permute-start | bytes 1544 | tf_op jit(solution)/shard_map/ppermute | solution.py:12
  92.2 409.3 %collective-permute-start.10 = (f32[1,2,64]{2,1,0:T(2,128)}, f32[1,2,64]{2,1,0:T(2,128)}, u32[]{:S(2)}, u32[]{:S(2)}) collective-permute-start(f32[1,2,64]{2,1,0:T(2,128)} %get-tuple-element.48), channel_id=1, source_target_pairs={{8,0},{12,4},{16,8},{20,12},{24,16},{28,20},{0,24},{4,28},{9,1},{1... | collective-permute-start | bytes 1544 | tf_op jit(solution)/shard_map/ppermute | solution.py:12
  94.6 392.2 %collective-permute-start.6 = (f32[1,2,64]{2,1,0:T(2,128)}, f32[1,2,64]{2,1,0:T(2,128)}, u32[]{:S(2)}, u32[]{:S(2)}) collective-permute-start(f32[1,2,64]{2,1,0:T(2,128)} %get-tuple-element.52), channel_id=1, source_target_pairs={{28,0},{0,4},{4,8},{8,12},{12,16},{16,20},{20,24},{24,28},{29,1},{... | collective-permute-start | bytes 1544 | tf_op jit(solution)/shard_map/ppermute | solution.py:12
  433.7 32.9 %copy-start = (f32[10,3072]{1,0:T(8,128)S(1)}, f32[10,3072]{1,0:T(8,128)}, u32[]{:S(2)}) copy-start(f32[10,3072]{1,0:T(8,128)} %param.20) | copy-start | bytes 368644
  466.6 20.2 %copy-start.3 = (f32[1,2,64]{2,1,0:T(2,128)S(1)}, f32[1,2,64]{2,1,0:T(2,128)}, u32[]{:S(2)}) copy-start(f32[1,2,64]{2,1,0:T(2,128)} %get-tuple-element.51) | copy-start | bytes 1540
  466.6 25.6 %copy-start.2 = (f32[1,2,64]{2,1,0:T(2,128)S(1)}, f32[1,2,64]{2,1,0:T(2,128)}, u32[]{:S(2)}) copy-start(f32[1,2,64]{2,1,0:T(2,128)} %get-tuple-element.50) | copy-start | bytes 1540
  466.6 31.0 %copy-start.1 = (f32[1,2,64]{2,1,0:T(2,128)S(1)}, f32[1,2,64]{2,1,0:T(2,128)}, u32[]{:S(2)}) copy-start(f32[1,2,64]{2,1,0:T(2,128)} %get-tuple-element.49) | copy-start | bytes 1540
  486.8 5.4 %collective-permute-start.7 = (f32[1,2,64]{2,1,0:T(2,128)S(1)}, f32[1,2,64]{2,1,0:T(2,128)S(1)}, u32[]{:S(2)}, u32[]{:S(2)}) collective-permute-start(f32[1,2,64]{2,1,0:T(2,128)S(1)} %copy-done.3), channel_id=1, source_target_pairs={{24,0},{28,4},{0,8},{4,12},{8,16},{12,20},{16,24},{20,28},{25,1},{... | collective-permute-start | bytes 1544 | tf_op jit(solution)/shard_map/ppermute | solution.py:12
  492.2 5.4 %collective-permute-start.8 = (f32[1,2,64]{2,1,0:T(2,128)S(1)}, f32[1,2,64]{2,1,0:T(2,128)S(1)}, u32[]{:S(2)}, u32[]{:S(2)}) collective-permute-start(f32[1,2,64]{2,1,0:T(2,128)S(1)} %copy-done.2), channel_id=1, source_target_pairs={{20,0},{24,4},{28,8},{0,12},{4,16},{8,20},{12,24},{16,28},{21,1},{... | collective-permute-start | bytes 1544 | tf_op jit(solution)/shard_map/ppermute | solution.py:12
  497.6 3.9 collective-permute-start.9
where the time goes:
time: 537 us; the launch traced here: 528 us
  local copies, waits for them, and re-layouts  413 us (77%)
  other arithmetic  68.5 us (13%)
  waiting for transfers between devices  22.6 us (4%)
  starting transfers between devices  22.5 us (4%)
    gather x6, local copies, waits for them, and re-layouts, lookup(): jnp.take(field, table.reshape(-1), axis=1)  382 us
    select_n x4, other arithmetic, lookup(): jnp.take(field, table.reshape(-1), axis=1)  33 us
    ppermute x12, waiting for transfers between devices, from_behind(): return lax.ppermute(block, axis, route)  22.6 us
    ppermute x12, starting transfers between devices, from_behind(): return lax.ppermute(block, axis, route)  17.5 us
    reduce_sum x1, other arithmetic, body(): tangent = jnp.sum(weights_on_edge * speed_near, axis=1)  17.2 us
  transfers between devices with their start and end apart: 14, of which 6 were waited for; matrix products, arithmetic and copies ran while one was open for 91% of the time, Pallas kernels for 0%

commit v1 on v0

v1 whole, which is shorter than its diff:
```python
import functools

import jax
import jax.numpy as jnp
from jax import lax
from jax.experimental import pallas as pl
from jax.experimental.pallas import tpu as pltpu
from jax.sharding import PartitionSpec as P

MESH = pl.DeviceIdType.MESH
LANES = 128
SUB = 8
ALONG_LANES = lax.GatherDimensionNumbers(
    offset_dims=(),
    collapsed_slice_dims=(1,),
    start_index_map=(1,),
    operand_batching_dims=(0,),
    start_indices_batching_dims=(0,),
)


def pick(row, lanes):
    return lax.gather(
        row,
        lanes[..., None],
        ALONG_LANES,
        slice_sizes=(1, 1),
        mode=lax.GatherScatterMode.PROMISE_IN_BOUNDS,
    )


def tile(c):
    return pl.ds(pl.multiple_of(c * LANES, LANES), LANES)


def spread(row):
    return jnp.broadcast_to(row, (SUB, LANES))


def scan(first, last, load_rows, lookups, found, unroll):
    def step(k, found):
        rows = load_rows(k)
        after = []
        for (row_of, lane_of), held in zip(lookups, found):
            hit = row_of == k
            after.append(tuple(jnp.where(hit, pick(r, lane_of), h) for r, h in zip(rows, held)))
        return tuple(after)

    return lax.fori_loop(first, last, step, tuple(found), unroll=unroll)


def total_rows(x):
    return jnp.sum(x, axis=0, keepdims=True)


def kernel(
    n_mesh,
    n_lev,
    vel_h, thk_h, vor_h, wind_h, wts_h, eoe_h, eoc_h, coe_h, ew_h, invd_h, ehl_h, ehc_h, chl_h, chc_h,
    tend, tang, energy,
    vel, thk, vor, wind, wts, eoe, eoc, coe, ew, invd, ehl, ehc, chl, chc,
    below, above, esend, erecv, csend, crecv, near, cell_near, cell_pick,
    load_sem, es_sem, er_sem, cs_sem, cr_sem, ls_sem, lr_sem,
):
    levels, edges = vel.shape
    cells = energy.shape[1]
    blocks = ehl.shape[0]
    reach = blocks // 2
    halo_c = chl.shape[1]
    neoe, neoc = eoe.shape[0], eoc.shape[0]
    extra = neoe - SUB
    group = SUB // extra
    units = edges // (LANES * group)
    edge_rows = edges // LANES
    cell_rows = cells // LANES
    planes = 3 * levels
    me = lax.axis_index("mesh")
    lev = lax.axis_index("lev")

    def partner(o):
        offset = o + 1 if o < reach else reach - 1 - o
        return {"mesh": lax.rem(me + offset + n_mesh, n_mesh)}

    up = {"lev": lax.rem(lev + 1, n_lev)}
    down = {"lev": lax.rem(lev + n_lev - 1, n_lev)}

    barrier = pltpu.get_barrier_semaphore()
    for o in range(blocks):
        pl.semaphore_signal(barrier, inc=1, device_id=partner(o), device_id_type=MESH)
    pl.semaphore_signal(barrier, inc=1, device_id=up, device_id_type=MESH)
    pl.semaphore_signal(barrier, inc=1, device_id=down, device_id_type=MESH)

    pairs = [
        (ehl_h, ehl), (ehc_h, ehc), (vel_h, vel), (thk_h, thk), (vor_h, vor),
        (eoc_h, eoc), (eoe_h, eoe), (ew_h, ew), (wts_h, wts), (chl_h, chl), (chc_h, chc),
        (coe_h, coe), (invd_h, invd), (wind_h, wind),
    ]
    loads = []
    for i, (src, dst) in enumerate(pairs):
        copy = pltpu.make_async_copy(src, dst, load_sem.at[i])
        copy.start()
        loads.append(copy)
    esend[...] = jnp.zeros_like(esend)
    csend[...] = jnp.zeros_like(csend)
    cell_pick[...] = jnp.zeros_like(cell_pick)

    sublane = lax.broadcasted_iota(jnp.int32, (SUB, LANES), 0)
    lane = lax.broadcasted_iota(jnp.int32, (SUB, LANES), 1)
    blank = jnp.zeros((SUB, LANES), jnp.float32)

    def live(counts):
        most = jnp.zeros((SUB, LANES), jnp.int32)
        for o in range(blocks):
            most = jnp.where(sublane == o, counts[o], most)
        return lane < most

    def field_rows(k):
        return [
            spread(field[l : l + 1, tile(k)]) for field in (vel, thk, vor) for l in range(levels)
        ]

    def speed_rows(k):
        return [spread(vel[l : l + 1, tile(k)]) for l in range(levels)]

    def padded_rows(x):
        return jnp.concatenate([x, jnp.zeros((SUB - x.shape[0], LANES), x.dtype)], axis=0)

    for copy in loads[:5]:
        copy.wait()
    index = padded_rows(ehl[...])
    (packed,) = scan(
        0, edge_rows, field_rows, [(index >> 7, index & 127)], [(blank,) * planes], 4
    )
    alive = live(ehc)
    for p in range(planes):
        block = jnp.where(alive, packed[p], 0.0)
        for o in range(blocks):
            esend[SUB * o + p : SUB * o + p + 1, :] = block[o : o + 1]

    pl.semaphore_wait(barrier, blocks + 2)
    edge_copies = []
    for o in range(blocks):
        rows = pl.ds(SUB * o, SUB)
        copy = pltpu.make_async_remote_copy(
            src_ref=esend.at[rows],
            dst_ref=erecv.at[rows],
            send_sem=es_sem.at[o],
            recv_sem=er_sem.at[o],
            device_id=partner(o),
            device_id_type=MESH,
        )
        copy.start()
        edge_copies.append(copy)
    rim_copies = []
    for i, (dst, target) in enumerate(((below, up), (above, down))):
        copy = pltpu.make_async_remote_copy(
            src_ref=vel,
            dst_ref=dst,
            send_sem=ls_sem.at[i],
            recv_sem=lr_sem.at[i],
            device_id=target,
            device_id_type=MESH,
        )
        copy.start()
        rim_copies.append(copy)

    loads[5].wait()
    cell_lookups = []
    for c in range(cell_rows):
        index = padded_rows(eoc[:, c * LANES : (c + 1) * LANES])
        cell_lookups.append((index >> 7, index & 127))
    found = scan(
        0, edge_rows, speed_rows, cell_lookups, [(blank,) * levels] * cell_rows, 1
    )
    for c in range(cell_rows):
        for l in range(levels):
            cell_near[c * levels + l] = found[c][l]

    loads[6].wait()

    def unit_lookups(u):
        lookups = []
        for q in range(group):
            index = eoe[0:SUB, tile(u * group + q)]
            lookups.append((index >> 7, index & 127))
        index = jnp.concatenate(
            [eoe[SUB:neoe, tile(u * group + q)] for q in range(group)], axis=0
        )
        lookups.append((index >> 7, index & 127))
        return lookups

    def local_unit(u, carry):
        found = scan(
            0, edge_rows, field_rows, unit_lookups(u), [(blank,) * planes] * (group + 1), 2
        )
        for g in range(group + 1):
            for p in range(planes):
                near[u, g * planes + p] = found[g][p]
        return carry

    lax.fori_loop(0, units, local_unit, 0)

    for copy in edge_copies:
        copy.wait()
    loads[7].wait()

    def halo_rows(count):
        def load(k):
            start = pl.multiple_of(SUB * (k - edge_rows), SUB)
            rows = erecv[pl.ds(start, SUB), :]
            return [spread(rows[p : p + 1]) for p in range(count)]

        return load

    found = [
        tuple(cell_near[c * levels + l] for l in range(levels)) for c in range(cell_rows)
    ]
    found = scan(edge_rows, edge_rows + blocks, halo_rows(levels), cell_lookups, found, 1)
    for c in range(cell_rows):
        weight = padded_rows(ew[:, c * LANES : (c + 1) * LANES])
        energy[:, c * LANES : (c + 1) * LANES] = jnp.concatenate(
            [total_rows(weight * found[c][l] * found[c][l]) for l in range(levels)], axis=0
        )

    for copy in loads[9:11]:
        copy.wait()
    cell_pick[0:blocks, 0:halo_c] = chl[...]
    index = cell_pick[...]

    def energy_rows(k):
        return [spread(energy[l : l + 1, tile(k)]) for l in range(levels)]

    (packed,) = scan(
        0, cell_rows, energy_rows, [(index >> 7, index & 127)], [(blank,) * levels], cell_rows
    )
    alive = live(chc)
    for l in range(levels):
        block = jnp.where(alive, packed[l], 0.0)
        for o in range(blocks):
            csend[SUB * o + l : SUB * o + l + 1, :] = block[o : o + 1]
    cell_copies = []
    for o in range(blocks):
        rows = pl.ds(SUB * o, SUB)
        copy = pltpu.make_async_remote_copy(
            src_ref=csend.at[rows],
            dst_ref=crecv.at[rows],
            send_sem=cs_sem.at[o],
            recv_sem=cr_sem.at[o],
            device_id=partner(o),
            device_id_type=MESH,
        )
        copy.start()
        cell_copies.append(copy)

    loads[8].wait()

    def halo_unit(u, carry):
        found = [
            tuple(near[u, g * planes + p] for p in range(planes)) for g in range(group + 1)
        ]
        found = scan(
            edge_rows, edge_rows + blocks, halo_rows(planes), unit_lookups(u), found, 1
        )
        cols = [tile(u * group + q) for q in range(group)]
        few = jnp.concatenate([wts[SUB:neoe, c] for c in cols], axis=0)
        tangents = [[] for _ in cols]
        fluxes = [[] for _ in cols]
        for l in range(levels):
            own = [vor[l : l + 1, c] for c in cols]
            speed, height, potential = (found[group][f * levels + l] for f in range(3))
            own_few = jnp.concatenate(
                [jnp.broadcast_to(v, (extra, LANES)) for v in own], axis=0
            )
            moved_few = few * speed
            flux_few = moved_few * height * 0.5 * (own_few + potential)
            for q, c in enumerate(cols):
                speed, height, potential = (found[q][f * levels + l] for f in range(3))
                moved = wts[0:SUB, c] * speed
                flux = moved * height * 0.5 * (spread(own[q]) + potential)
                part = slice(extra * q, extra * (q + 1))
                tangents[q].append(total_rows(moved) + total_rows(moved_few[part]))
                fluxes[q].append(total_rows(flux) + total_rows(flux_few[part]))
        for q, c in enumerate(cols):
            tang[:, c] = jnp.concatenate(tangents[q], axis=0)
            tend[:, c] = jnp.concatenate(fluxes[q], axis=0)
        return carry

    lax.fori_loop(0, units, halo_unit, 0)

    for copy in cell_copies + rim_copies + loads[11:]:
        copy.wait()
    ends = SUB // 2

    def end_unit(u, carry):
        cols = [tile(u * ends + q) for q in range(ends)]
        index = jnp.concatenate([coe[:, c] for c in cols], axis=0)
        far = index >= cells
        slot = index - cells
        place = (
            jnp.where(far, cell_rows + slot // halo_c, index >> 7),
            jnp.where(far, slot % halo_c, index & 127),
        )

        def received_rows(k):
            start = pl.multiple_of(SUB * (k - cell_rows), SUB)
            rows = crecv[pl.ds(start, SUB), :]
            return [spread(rows[l : l + 1]) for l in range(levels)]

        found = scan(0, cell_rows, energy_rows, [place], [(blank,) * levels], cell_rows)
        (found,) = scan(cell_rows, cell_rows + blocks, received_rows, [place], found, blocks)
        for q, c in enumerate(cols):
            rows = []
            for l in range(levels):
                gradient = (
                    found[l][2 * q + 1 : 2 * q + 2] - found[l][2 * q : 2 * q + 1]
                ) * invd[pl.ds(u * ends + q, 1), :]
                if l + 1 < levels:
                    over = vel[l + 1 : l + 2, c]
                else:
                    over = jnp.where(lev == n_lev - 1, 0.0, above[0:1, c])
                if l > 0:
                    under = vel[l - 1 : l, c]
                else:
                    under = jnp.where(lev == 0, 0.0, below[levels - 1 : levels, c])
                advect = -0.5 * wind[l : l + 1, c] * (over - under)
                rows.append((tend[l : l + 1, c] - gradient) + advect)
            tend[:, c] = jnp.concatenate(rows, axis=0)
        return carry

    lax.fori_loop(0, edge_rows // ends, end_unit, 0)


def body(
    velocity,
    thickness,
    vorticity,
    vertical_wind,
    weights_on_edge,
    edges_on_edge,
    edges_on_cell,
    cells_on_edge,
    energy_weight,
    inverse_distance,
    edge_halo_list,
    edge_halo_count,
    cell_halo_list,
    cell_halo_count,
):
    levels, edges = velocity.shape
    cells = edges_on_cell.shape[1]
    blocks = edge_halo_list.shape[0]
    group = SUB // (edges_on_edge.shape[0] - SUB)
    units = edges // (LANES * group)
    args = [
        velocity, thickness, vorticity, vertical_wind, weights_on_edge, edges_on_edge,
        edges_on_cell, cells_on_edge, energy_weight, inverse_distance.reshape(-1, LANES),
        edge_halo_list, edge_halo_count, cell_halo_list, cell_halo_count,
    ]
    held = [
        pltpu.SMEM(a.shape, a.dtype) if a.ndim == 1 else pltpu.VMEM(a.shape, a.dtype) for a in args
    ]
    exchange = pltpu.VMEM((SUB * blocks, LANES), jnp.float32)
    dma = lambda n: pltpu.SemaphoreType.DMA((n,))
    return pl.pallas_call(
        functools.partial(kernel, lax.axis_size("mesh"), lax.axis_size("lev")),
        out_shape=(
            jax.ShapeDtypeStruct((levels, edges), jnp.float32),
            jax.ShapeDtypeStruct((levels, edges), jnp.float32),
            jax.ShapeDtypeStruct((levels, cells), jnp.float32),
        ),
        in_specs=[pl.BlockSpec(memory_space=pl.ANY)] * len(args),
        out_specs=(pl.BlockSpec(memory_space=pltpu.VMEM),) * 3,
        scratch_shapes=held
        + [
            pltpu.VMEM((levels, edges), jnp.float32),
            pltpu.VMEM((levels, edges), jnp.float32),
            exchange, exchange, exchange, exchange,
            pltpu.VMEM((units, (group + 1) * 3 * levels, SUB, LANES), jnp.float32),
            pltpu.VMEM((cells // LANES * levels, SUB, LANES), jnp.float32),
            pltpu.VMEM((SUB, LANES), jnp.int32),
            dma(len(args)), dma(blocks), dma(blocks), dma(blocks), dma(blocks), dma(2), dma(2),
        ],
        compiler_params=pltpu.CompilerParams(collective_id=0, has_side_effects=True),
    )(*args)


def solution(mesh):
    in_specs = (
        P("lev", "mesh"),
        P("lev", "mesh"),
        P("lev", "mesh"),
        P("lev", "mesh"),
        P(None, "mesh"),
        P(None, "mesh"),
        P(None, "mesh"),
        P(None, "mesh"),
        P(None, "mesh"),
        P("mesh"),
        P("mesh", None),
        P("mesh"),
        P("mesh", None),
        P("mesh"),
    )
    out_specs = (P("lev", "mesh"), P("lev", "mesh"), P("lev", "mesh"))
    return jax.shard_map(body, mesh=mesh, in_specs=in_specs, out_specs=out_specs, check_vma=False)
```

time: 537 us -> 30.8 us (0.06); the launches traced: 528 us -> 30.5 us
  local copies, waits for them, and re-layouts: 413 us -> 2.66 us
  other arithmetic: 68.5 us -> 0 us
  Pallas kernels: 0 us -> 27.2 us
  waiting for transfers between devices: 22.6 us -> 0 us
  starting transfers between devices: 22.5 us -> 0 us
    gather x10 -> x0, local copies, waits for them, and re-layouts: 391 us -> none  [the longest x6 382 us: lookup(): jnp.take(field, table.reshape(-1), axis=1)]
    select_n x8 -> x0, other arithmetic: 34.4 us -> none  [the longest x4 33 us: lookup(): jnp.take(field, table.reshape(-1), axis=1)]
    pallas_call x0 -> x1, Pallas kernels: none -> 27.2 us  [body(): pl.pallas_call(functools.partial(kernel, lax.axis_size('mesh'), lax.axis_...]
    reduce_sum x2 -> x0, other arithmetic: 22.7 us -> none  [the longest x1 17.2 us: body(): tangent = jnp.sum(weights_on_edge * speed_near, axis=1)]
    ppermute x14 -> x0, waiting for transfers between devices: 22.6 us -> none  [the longest x12 22.6 us: from_behind(): return lax.ppermute(block, axis, route)]
    ppermute x14 -> x0, starting transfers between devices: 22.5 us -> none  [the longest x12 17.5 us: from_behind(): return lax.ppermute(block, axis, route)]
    squeeze x6 -> x0, local copies, waits for them, and re-layouts: 7.14 us -> none  [the longest x1 2.64 us: body(): potential_near = lookup(extended[2], edges_on_edge)]
    unnamed x23 -> x7, local copies, waits for them, and re-layouts: 8.47 us -> 2.66 us
  transfers between devices with their start and end apart: 14 -> 0, of which waited for: 6 -> 0; matrix products, arithmetic and copies ran while one was open for 91% -> 0% of each run, Pallas kernels for 0% -> 0%
where the time goes in v1:
time: 30.8 us; the launch traced here: 30.5 us
  Pallas kernels  27.2 us (88%)
  local copies, waits for them, and re-layouts  2.66 us (9%)
  between operations  0.65 us (2%)
    pallas_call x1, Pallas kernels, body(): pl.pallas_call(functools.partial(kernel, lax.axis_size('mesh'), lax.axis_...  27.2 us
    unnamed x7, local copies, waits for them, and re-layouts  2.66 us

profile of v1, /device:TPU:0, one launch (start us, length us, event | category | flops | bytes accessed | tf_op | source)
XLA Modules:
  0.0 30.5 jit_solution(14284750564234419601)
XLA Ops:
  0.6 27.2 %shard_map.157 = (f32[2,3072]{1,0:T(2,128)}, f32[2,3072]{1,0:T(2,128)}, f32[2,1024]{1,0:T(2,128)}) custom-call(f32[2,3072]{1,0:T(2,128)} %vel_h.1, f32[2,3072]{1,0:T(2,128)} %thk_h.1, f32[2,3072]{1,0:T(2,128)} %vor_h.1, f32[2,3072]{1,0:T(2,128)} %wind_h.1, f32[10,3072]{1,0:T(8,128)} %wts_h.1, s32[10,3072]{1,0:T(8,128)} %eoe_h.1, s32[6,1024]{1,0:T(8,128)} %eoc_h.1, ...), custom_call_target="tpu_custom_call" | custom-call | tf_op jit(solution)/shard_map/pallas_call | solution.py:364
  27.9 0.0 copy-start
  27.9 1.4 %copy.20 = f32[2,3072]{1,0:T(2,128)} copy(f32[2,3072]{1,0:T(2,128)} %get-tuple-element.6) | data formatting | bytes 49152
  29.2 0.0 copy-done
  29.2 0.0 copy-start.1
  29.2 0.6 %copy.21 = f32[2,3072]{1,0:T(2,128)} copy(f32[2,3072]{1,0:T(2,128)S(1)} %copy-done) | data formatting | bytes 49152
  29.8 0.1 copy-done.1
  29.9 0.6 %copy.22 = f32[2,1024]{1,0:T(2,128)} copy(f32[2,1024]{1,0:T(2,128)S(1)} %copy-done.1) | data formatting | bytes 16384
Async XLA Ops:
  27.9 1.4 %copy-start = (f32[2,3072]{1,0:T(2,128)S(1)}, f32[2,3072]{1,0:T(2,128)}, u32[]{:S(2)}) copy-start(f32[2,3072]{1,0:T(2,128)} %get-tuple-element.7) | copy-start | bytes 73732
  29.2 0.7 %copy-start.1 = (f32[2,1024]{1,0:T(2,128)S(1)}, f32[2,1024]{1,0:T(2,128)}, u32[]{:S(2)}) copy-start(f32[2,1024]{1,0:T(2,128)} %get-tuple-element.8) | copy-start | bytes 24580

commit v2 on v1

--- a/solution.py
+++ b/solution.py
@@ -129,7 +129,7 @@
         copy.wait()
     index = padded_rows(ehl[...])
     (packed,) = scan(
-        0, edge_rows, field_rows, [(index >> 7, index & 127)], [(blank,) * planes], 4
+        0, edge_rows, field_rows, [(index >> 7, index & 127)], [(blank,) * planes], edge_rows
     )
     alive = live(ehc)
     for p in range(planes):
@@ -170,7 +170,7 @@
         index = padded_rows(eoc[:, c * LANES : (c + 1) * LANES])
         cell_lookups.append((index >> 7, index & 127))
     found = scan(
-        0, edge_rows, speed_rows, cell_lookups, [(blank,) * levels] * cell_rows, 1
+        0, edge_rows, speed_rows, cell_lookups, [(blank,) * levels] * cell_rows, edge_rows
     )
     for c in range(cell_rows):
         for l in range(levels):
@@ -191,7 +191,7 @@
 
     def local_unit(u, carry):
         found = scan(
-            0, edge_rows, field_rows, unit_lookups(u), [(blank,) * planes] * (group + 1), 2
+            0, edge_rows, field_rows, unit_lookups(u), [(blank,) * planes] * (group + 1), edge_rows
         )
         for g in range(group + 1):
             for p in range(planes):
@@ -215,7 +215,7 @@
     found = [
         tuple(cell_near[c * levels + l] for l in range(levels)) for c in range(cell_rows)
     ]
-    found = scan(edge_rows, edge_rows + blocks, halo_rows(levels), cell_lookups, found, 1)
+    found = scan(edge_rows, edge_rows + blocks, halo_rows(levels), cell_lookups, found, blocks)
     for c in range(cell_rows):
         weight = padded_rows(ew[:, c * LANES : (c + 1) * LANES])
         energy[:, c * LANES : (c + 1) * LANES] = jnp.concatenate(
@@ -259,7 +259,7 @@
             tuple(near[u, g * planes + p] for p in range(planes)) for g in range(group + 1)
         ]
         found = scan(
-            edge_rows, edge_rows + blocks, halo_rows(planes), unit_lookups(u), found, 1
+            edge_rows, edge_rows + blocks, halo_rows(planes), unit_lookups(u), found, blocks
         )
         cols = [tile(u * group + q) for q in range(group)]
         few = jnp.concatenate([wts[SUB:neoe, c] for c in cols], axis=0)

time: 30.8 us -> 22.9 us (0.74)
  Pallas kernels: 27.2 us -> 19.3 us
    pallas_call x1, Pallas kernels: 27.2 us -> 19.3 us  [body(): pl.pallas_call(functools.partial(kernel, lax.axis_size('mesh'), lax.axis_...]
where the time goes in v2:
time: 22.9 us; the launch traced here: 22.6 us
  Pallas kernels  19.3 us (84%)
  local copies, waits for them, and re-layouts  2.66 us (12%)
  between operations  0.65 us (3%)
    pallas_call x1, Pallas kernels, body(): pl.pallas_call(functools.partial(kernel, lax.axis_size('mesh'), lax.axis_...  19.3 us
    unnamed x7, local copies, waits for them, and re-layouts  2.66 us

profile of v2, /device:TPU:0, one launch (start us, length us, event | category | flops | bytes accessed | tf_op | source)
XLA Modules:
  0.0 22.6 jit_solution(2064934873447464971)
XLA Ops:
  0.6 19.3 %shard_map.157 = (f32[2,3072]{1,0:T(2,128)}, f32[2,3072]{1,0:T(2,128)}, f32[2,1024]{1,0:T(2,128)}) custom-call(f32[2,3072]{1,0:T(2,128)} %vel_h.1, f32[2,3072]{1,0:T(2,128)} %thk_h.1, f32[2,3072]{1,0:T(2,128)} %vor_h.1, f32[2,3072]{1,0:T(2,128)} %wind_h.1, f32[10,3072]{1,0:T(8,128)} %wts_h.1, s32[10,3072]{1,0:T(8,128)} %eoe_h.1, s32[6,1024]{1,0:T(8,128)} %eoc_h.1, ...), custom_call_target="tpu_custom_call" | custom-call | tf_op jit(solution)/shard_map/pallas_call | solution.py:364
  20.0 0.0 copy-start
  20.0 1.4 %copy.20 = f32[2,3072]{1,0:T(2,128)} copy(f32[2,3072]{1,0:T(2,128)} %get-tuple-element.6) | data formatting | bytes 49152
  21.3 0.0 copy-done
  21.3 0.0 copy-start.1
  21.3 0.6 %copy.21 = f32[2,3072]{1,0:T(2,128)} copy(f32[2,3072]{1,0:T(2,128)S(1)} %copy-done) | data formatting | bytes 49152
  21.9 0.1 copy-done.1
  22.0 0.6 %copy.22 = f32[2,1024]{1,0:T(2,128)} copy(f32[2,1024]{1,0:T(2,128)S(1)} %copy-done.1) | data formatting | bytes 16384
Async XLA Ops:
  20.0 1.4 %copy-start = (f32[2,3072]{1,0:T(2,128)S(1)}, f32[2,3072]{1,0:T(2,128)}, u32[]{:S(2)}) copy-start(f32[2,3072]{1,0:T(2,128)} %get-tuple-element.7) | copy-start | bytes 73732
  21.3 0.7 %copy-start.1 = (f32[2,1024]{1,0:T(2,128)S(1)}, f32[2,1024]{1,0:T(2,128)}, u32[]{:S(2)}) copy-start(f32[2,1024]{1,0:T(2,128)} %get-tuple-element.8) | copy-start | bytes 24580

commit v3 on v2

--- a/solution.py
+++ b/solution.py
@@ -57,10 +57,10 @@
     n_mesh,
     n_lev,
     vel_h, thk_h, vor_h, wind_h, wts_h, eoe_h, eoc_h, coe_h, ew_h, invd_h, ehl_h, ehc_h, chl_h, chc_h,
-    tend, tang, energy,
+    tend_h, tang_h, energy_h,
     vel, thk, vor, wind, wts, eoe, eoc, coe, ew, invd, ehl, ehc, chl, chc,
-    below, above, esend, erecv, csend, crecv, near, cell_near, cell_pick,
-    load_sem, es_sem, er_sem, cs_sem, cr_sem, ls_sem, lr_sem,
+    tend, tang, energy, below, above, esend, erecv, csend, crecv, near, cell_near, cell_pick,
+    load_sem, es_sem, er_sem, cs_sem, cr_sem, ls_sem, lr_sem, out_sem,
 ):
     levels, edges = vel.shape
     cells = energy.shape[1]
@@ -221,6 +221,9 @@
         energy[:, c * LANES : (c + 1) * LANES] = jnp.concatenate(
             [total_rows(weight * found[c][l] * found[c][l]) for l in range(levels)], axis=0
         )
+
+    energy_out = pltpu.make_async_copy(energy, energy_h, out_sem.at[0])
+    energy_out.start()
 
     for copy in loads[9:11]:
         copy.wait()
@@ -285,7 +288,9 @@
             tend[:, c] = jnp.concatenate(fluxes[q], axis=0)
         return carry
 
-    lax.fori_loop(0, units, halo_unit, 0)
+    lax.fori_loop(0, units, halo_unit, 0, unroll=2)
+    tang_out = pltpu.make_async_copy(tang, tang_h, out_sem.at[1])
+    tang_out.start()
 
     for copy in cell_copies + rim_copies + loads[11:]:
         copy.wait()
@@ -327,7 +332,23 @@
             tend[:, c] = jnp.concatenate(rows, axis=0)
         return carry
 
-    lax.fori_loop(0, edge_rows // ends, end_unit, 0)
+    lax.fori_loop(0, edge_rows // ends, end_unit, 0, unroll=edge_rows // ends)
+    tend_out = pltpu.make_async_copy(tend, tend_h, out_sem.at[2])
+    tend_out.start()
+    for copy in (energy_out, tang_out, tend_out):
+        copy.wait()
+
+
+def place(*refs):
+    *pairs, sem = refs
+    half = len(pairs) // 2
+    copies = [
+        pltpu.make_async_copy(pairs[i], pairs[half + i], sem.at[i]) for i in range(half)
+    ]
+    for copy in copies:
+        copy.start()
+    for copy in copies:
+        copy.wait()
 
 
 def body(
@@ -361,27 +382,39 @@
     ]
     exchange = pltpu.VMEM((SUB * blocks, LANES), jnp.float32)
     dma = lambda n: pltpu.SemaphoreType.DMA((n,))
-    return pl.pallas_call(
+    results = (
+        jax.ShapeDtypeStruct((levels, edges), jnp.float32),
+        jax.ShapeDtypeStruct((levels, edges), jnp.float32),
+        jax.ShapeDtypeStruct((levels, cells), jnp.float32),
+    )
+    anywhere = pl.BlockSpec(memory_space=pl.ANY)
+    found = pl.pallas_call(
         functools.partial(kernel, lax.axis_size("mesh"), lax.axis_size("lev")),
-        out_shape=(
-            jax.ShapeDtypeStruct((levels, edges), jnp.float32),
-            jax.ShapeDtypeStruct((levels, edges), jnp.float32),
-            jax.ShapeDtypeStruct((levels, cells), jnp.float32),
-        ),
-        in_specs=[pl.BlockSpec(memory_space=pl.ANY)] * len(args),
-        out_specs=(pl.BlockSpec(memory_space=pltpu.VMEM),) * 3,
+        out_shape=results,
+        in_specs=[anywhere] * len(args),
+        out_specs=(anywhere,) * 3,
         scratch_shapes=held
         + [
+            pltpu.VMEM((levels, edges), jnp.float32),
+            pltpu.VMEM((levels, edges), jnp.float32),
+            pltpu.VMEM((levels, cells), jnp.float32),
             pltpu.VMEM((levels, edges), jnp.float32),
             pltpu.VMEM((levels, edges), jnp.float32),
             exchange, exchange, exchange, exchange,
             pltpu.VMEM((units, (group + 1) * 3 * levels, SUB, LANES), jnp.float32),
             pltpu.VMEM((cells // LANES * levels, SUB, LANES), jnp.float32),
             pltpu.VMEM((SUB, LANES), jnp.int32),
-            dma(len(args)), dma(blocks), dma(blocks), dma(blocks), dma(blocks), dma(2), dma(2),
+            dma(len(args)), dma(blocks), dma(blocks), dma(blocks), dma(blocks), dma(2), dma(2), dma(3),
         ],
         compiler_params=pltpu.CompilerParams(collective_id=0, has_side_effects=True),
     )(*args)
+    return pl.pallas_call(
+        place,
+        out_shape=results,
+        in_specs=[anywhere] * 3,
+        out_specs=(anywhere,) * 3,
+        scratch_shapes=[dma(3)],
+    )(*found)
 
 
 def solution(mesh):

time: 22.9 us -> 22.5 us (0.983)
  local copies, waits for them, and re-layouts: 2.66 us -> 0 us
  Pallas kernels: 19.3 us -> 21.6 us
    pallas_call x0 -> x1, Pallas kernels: none -> 2.87 us  [body(): pl.pallas_call(place, out_shape=results, in_specs=[anywhere] * 3, out_spe...]
    unnamed x7 -> x0, local copies, waits for them, and re-layouts: 2.66 us -> none
    pallas_call x1, Pallas kernels: 19.3 us -> 18.8 us  [body(): pl.pallas_call(functools.partial(kernel, lax.axis_size('mesh'), lax.axis_...]
where the time goes in v3:
time: 22.5 us; the launch traced here: 22.3 us
  Pallas kernels  21.6 us (96%)
  between operations  0.64 us (3%)
    pallas_call x1, Pallas kernels, body(): pl.pallas_call(functools.partial(kernel, lax.axis_size('mesh'), lax.axis_...  18.8 us
    pallas_call x1, Pallas kernels, body(): pl.pallas_call(place, out_shape=results, in_specs=[anywhere] * 3, out_spe...  2.87 us

profile of v3, /device:TPU:0, one launch (start us, length us, event | category | flops | bytes accessed | tf_op | source)
XLA Modules:
  0.0 22.3 jit_solution(17431534367256756062)
XLA Ops:
  0.6 18.8 %shard_map.157 = (f32[2,3072]{1,0:T(2,128)}, f32[2,3072]{1,0:T(2,128)}, f32[2,1024]{1,0:T(2,128)}) custom-call(f32[2,3072]{1,0:T(2,128)} %vel_h.1, f32[2,3072]{1,0:T(2,128)} %thk_h.1, f32[2,3072]{1,0:T(2,128)} %vor_h.1, f32[2,3072]{1,0:T(2,128)} %wind_h.1, f32[10,3072]{1,0:T(8,128)} %wts_h.1, s32[10,3072]{1,0:T(8,128)} %eoe_h.1, s32[6,1024]{1,0:T(8,128)} %eoc_h.1, ...), custom_call_target="tpu_custom_call" | custom-call | tf_op jit(solution)/shard_map/pallas_call | solution.py:391
  19.4 2.9 %shard_map.158 = (f32[2,3072]{1,0:T(2,128)}, f32[2,3072]{1,0:T(2,128)}, f32[2,1024]{1,0:T(2,128)}) custom-call(f32[2,3072]{1,0:T(2,128)} %get-tuple-element.6.refs_0_, f32[2,3072]{1,0:T(2,128)} %get-tuple-element.7.refs_1_, f32[2,1024]{1,0:T(2,128)} %get-tuple-element.8.refs_2_), custom_call_target="tpu_custom_call" | custom-call | tf_op jit(solution)/shard_map/pallas_call | solution.py:411

commit v4 on v3

--- a/solution.py
+++ b/solution.py
@@ -38,15 +38,16 @@
 
 
 def scan(first, last, load_rows, lookups, found, unroll):
-    def step(k, found):
-        rows = load_rows(k)
-        after = []
-        for (row_of, lane_of), held in zip(lookups, found):
+    def one(lookup, held):
+        row_of, lane_of = lookup
+
+        def step(k, held):
             hit = row_of == k
-            after.append(tuple(jnp.where(hit, pick(r, lane_of), h) for r, h in zip(rows, held)))
-        return tuple(after)
-
-    return lax.fori_loop(first, last, step, tuple(found), unroll=unroll)
+            return tuple(jnp.where(hit, pick(r, lane_of), h) for r, h in zip(load_rows(k), held))
+
+        return lax.fori_loop(first, last, step, tuple(held), unroll=unroll)
+
+    return tuple(one(lookup, held) for lookup, held in zip(lookups, found))
 
 
 def total_rows(x):
@@ -340,14 +341,17 @@
 
 
 def place(*refs):
-    *pairs, sem = refs
-    half = len(pairs) // 2
-    copies = [
-        pltpu.make_async_copy(pairs[i], pairs[half + i], sem.at[i]) for i in range(half)
-    ]
-    for copy in copies:
+    *arrays, in_sem, out_sem = refs
+    count = len(arrays) // 3
+    sources, targets, held = (arrays[i * count : (i + 1) * count] for i in range(3))
+    ins = [pltpu.make_async_copy(sources[i], held[i], in_sem.at[i]) for i in range(count)]
+    outs = [pltpu.make_async_copy(held[i], targets[i], out_sem.at[i]) for i in range(count)]
+    for copy in ins:
         copy.start()
-    for copy in copies:
+    for arrived, leaving in zip(ins, outs):
+        arrived.wait()
+        leaving.start()
+    for copy in outs:
         copy.wait()
 
 
@@ -413,7 +417,7 @@
         out_shape=results,
         in_specs=[anywhere] * 3,
         out_specs=(anywhere,) * 3,
-        scratch_shapes=[dma(3)],
+        scratch_shapes=[pltpu.VMEM(r.shape, r.dtype) for r in results] + [dma(3), dma(3)],
     )(*found)
 
 

time: 22.5 us -> 18.3 us (0.81)
  Pallas kernels: 21.6 us -> 17.4 us
    pallas_call x1, Pallas kernels: 18.8 us -> 16 us  [body(): pl.pallas_call(functools.partial(kernel, lax.axis_size('mesh'), lax.axis_...]
    pallas_call x1, Pallas kernels: 2.87 us -> 1.42 us  [body(): pl.pallas_call(place, out_shape=results, in_specs=[anywhere] * 3, out_spe...]
where the time goes in v4:
time: 18.3 us; the launch traced here: 18.1 us
  Pallas kernels  17.4 us (95%)
  between operations  0.64 us (3%)
    pallas_call x1, Pallas kernels, body(): pl.pallas_call(functools.partial(kernel, lax.axis_size('mesh'), lax.axis_...  16 us
    pallas_call x1, Pallas kernels, body(): pl.pallas_call(place, out_shape=results, in_specs=[anywhere] * 3, out_spe...  1.42 us

profile of v4, /device:TPU:0, one launch (start us, length us, event | category | flops | bytes accessed | tf_op | source)
XLA Modules:
  0.0 18.1 jit_solution(14200920623178686679)
XLA Ops:
  0.6 16.0 %shard_map.157 = (f32[2,3072]{1,0:T(2,128)}, f32[2,3072]{1,0:T(2,128)}, f32[2,1024]{1,0:T(2,128)}) custom-call(f32[2,3072]{1,0:T(2,128)} %vel_h.1, f32[2,3072]{1,0:T(2,128)} %thk_h.1, f32[2,3072]{1,0:T(2,128)} %vor_h.1, f32[2,3072]{1,0:T(2,128)} %wind_h.1, f32[10,3072]{1,0:T(8,128)} %wts_h.1, s32[10,3072]{1,0:T(8,128)} %eoe_h.1, s32[6,1024]{1,0:T(8,128)} %eoc_h.1, ...), custom_call_target="tpu_custom_call" | custom-call | tf_op jit(solution)/shard_map/pallas_call | solution.py:395
  16.6 1.4 %shard_map.158 = (f32[2,3072]{1,0:T(2,128)}, f32[2,3072]{1,0:T(2,128)}, f32[2,1024]{1,0:T(2,128)}) custom-call(f32[2,3072]{1,0:T(2,128)} %get-tuple-element.6.refs_0_, f32[2,3072]{1,0:T(2,128)} %get-tuple-element.7.refs_1_, f32[2,1024]{1,0:T(2,128)} %get-tuple-element.8.refs_2_), custom_call_target="tpu_custom_call" | custom-call | tf_op jit(solution)/shard_map/pallas_call | solution.py:415

commit v5 on v4

--- a/solution.py
+++ b/solution.py
@@ -9,6 +9,8 @@
 
 MESH = pl.DeviceIdType.MESH
 LANES = 128
+STEPS = 32767.0
+HALF = 1 << 16
 SUB = 8
 ALONG_LANES = lax.GatherDimensionNumbers(
     offset_dims=(),
@@ -50,6 +52,18 @@
     return tuple(one(lookup, held) for lookup, held in zip(lookups, found))
 
 
+def coded(low, high):
+    low, high = ((h * STEPS + 0.5).astype(jnp.int32) for h in (low, high))
+    return low + high * HALF
+
+
+def decoded(word):
+    return (
+        (word & (HALF - 1)).astype(jnp.float32),
+        lax.shift_right_logical(word, 16).astype(jnp.float32),
+    )
+
+
 def total_rows(x):
     return jnp.sum(x, axis=0, keepdims=True)
 
@@ -60,7 +74,7 @@
     vel_h, thk_h, vor_h, wind_h, wts_h, eoe_h, eoc_h, coe_h, ew_h, invd_h, ehl_h, ehc_h, chl_h, chc_h,
     tend_h, tang_h, energy_h,
     vel, thk, vor, wind, wts, eoe, eoc, coe, ew, invd, ehl, ehc, chl, chc,
-    tend, tang, energy, below, above, esend, erecv, csend, crecv, near, cell_near, cell_pick,
+    tend, tang, energy, below, above, esend, erecv, csend, crecv, near, near_code, code, code_halo, cell_near, cell_pick,
     load_sem, es_sem, er_sem, cs_sem, cr_sem, ls_sem, lr_sem, out_sem,
 ):
     levels, edges = vel.shape
@@ -75,6 +89,8 @@
     edge_rows = edges // LANES
     cell_rows = cells // LANES
     planes = 3 * levels
+    exact = 2 * levels
+    pairs_of = levels // 2
     me = lax.axis_index("mesh")
     lev = lax.axis_index("lev")
 
@@ -120,6 +136,10 @@
             spread(field[l : l + 1, tile(k)]) for field in (vel, thk, vor) for l in range(levels)
         ]
 
+    def table_rows(k):
+        rows = [spread(field[l : l + 1, tile(k)]) for field in (vel, vor) for l in range(levels)]
+        return rows + [spread(code[i : i + 1, tile(k)]) for i in range(pairs_of)]
+
     def speed_rows(k):
         return [spread(vel[l : l + 1, tile(k)]) for l in range(levels)]
 
@@ -165,6 +185,9 @@
         copy.start()
         rim_copies.append(copy)
 
+    for i in range(pairs_of):
+        code[i : i + 1, :] = coded(thk[2 * i : 2 * i + 1, :], thk[2 * i + 1 : 2 * i + 2, :])
+
     loads[5].wait()
     cell_lookups = []
     for c in range(cell_rows):
@@ -190,33 +213,48 @@
         lookups.append((index >> 7, index & 127))
         return lookups
 
+    none = (blank,) * exact + (jnp.zeros((SUB, LANES), jnp.int32),) * pairs_of
+
     def local_unit(u, carry):
         found = scan(
-            0, edge_rows, field_rows, unit_lookups(u), [(blank,) * planes] * (group + 1), edge_rows
+            0, edge_rows, table_rows, unit_lookups(u), [none] * (group + 1), edge_rows
         )
         for g in range(group + 1):
-            for p in range(planes):
-                near[u, g * planes + p] = found[g][p]
+            for p in range(exact):
+                near[u, g * exact + p] = found[g][p]
+            for i in range(pairs_of):
+                near_code[u, g * pairs_of + i] = found[g][exact + i]
         return carry
 
-    lax.fori_loop(0, units, local_unit, 0)
+    lax.fori_loop(0, units, local_unit, 0, unroll=2)
 
     for copy in edge_copies:
         copy.wait()
     loads[7].wait()
 
-    def halo_rows(count):
+    for o in range(blocks):
+        for i in range(pairs_of):
+            first = SUB * o + levels + 2 * i
+            code_halo[SUB * o + i : SUB * o + i + 1, :] = coded(
+                erecv[first : first + 1, :], erecv[first + 1 : first + 2, :]
+            )
+
+    def halo_rows(which, codes):
         def load(k):
             start = pl.multiple_of(SUB * (k - edge_rows), SUB)
             rows = erecv[pl.ds(start, SUB), :]
-            return [spread(rows[p : p + 1]) for p in range(count)]
+            taken = [spread(rows[p : p + 1]) for p in which]
+            if codes:
+                rows = code_halo[pl.ds(start, SUB), :]
+                taken += [spread(rows[i : i + 1]) for i in range(pairs_of)]
+            return taken
 
         return load
 
     found = [
         tuple(cell_near[c * levels + l] for l in range(levels)) for c in range(cell_rows)
     ]
-    found = scan(edge_rows, edge_rows + blocks, halo_rows(levels), cell_lookups, found, blocks)
+    found = scan(edge_rows, edge_rows + blocks, halo_rows(range(levels), False), cell_lookups, found, blocks)
     for c in range(cell_rows):
         weight = padded_rows(ew[:, c * LANES : (c + 1) * LANES])
         energy[:, c * LANES : (c + 1) * LANES] = jnp.concatenate(
@@ -258,29 +296,34 @@
 
     loads[8].wait()
 
+    table_halo = halo_rows(list(range(levels)) + list(range(2 * levels, planes)), True)
+
     def halo_unit(u, carry):
         found = [
-            tuple(near[u, g * planes + p] for p in range(planes)) for g in range(group + 1)
+            tuple(near[u, g * exact + p] for p in range(exact))
+            + tuple(near_code[u, g * pairs_of + i] for i in range(pairs_of))
+            for g in range(group + 1)
         ]
         found = scan(
-            edge_rows, edge_rows + blocks, halo_rows(planes), unit_lookups(u), found, blocks
-        )
+            edge_rows, edge_rows + blocks, table_halo, unit_lookups(u), found, blocks
+        )
+        heights = [sum((decoded(f[exact + i]) for i in range(pairs_of)), ()) for f in found]
         cols = [tile(u * group + q) for q in range(group)]
         few = jnp.concatenate([wts[SUB:neoe, c] for c in cols], axis=0)
         tangents = [[] for _ in cols]
         fluxes = [[] for _ in cols]
         for l in range(levels):
             own = [vor[l : l + 1, c] for c in cols]
-            speed, height, potential = (found[group][f * levels + l] for f in range(3))
+            speed, potential = found[group][l], found[group][levels + l]
             own_few = jnp.concatenate(
                 [jnp.broadcast_to(v, (extra, LANES)) for v in own], axis=0
             )
             moved_few = few * speed
-            flux_few = moved_few * height * 0.5 * (own_few + potential)
+            flux_few = moved_few * heights[group][l] * (0.5 / STEPS) * (own_few + potential)
             for q, c in enumerate(cols):
-                speed, height, potential = (found[q][f * levels + l] for f in range(3))
+                speed, potential = found[q][l], found[q][levels + l]
                 moved = wts[0:SUB, c] * speed
-                flux = moved * height * 0.5 * (spread(own[q]) + potential)
+                flux = moved * heights[q][l] * (0.5 / STEPS) * (spread(own[q]) + potential)
                 part = slice(extra * q, extra * (q + 1))
                 tangents[q].append(total_rows(moved) + total_rows(moved_few[part]))
                 fluxes[q].append(total_rows(flux) + total_rows(flux_few[part]))
@@ -289,7 +332,7 @@
             tend[:, c] = jnp.concatenate(fluxes[q], axis=0)
         return carry
 
-    lax.fori_loop(0, units, halo_unit, 0, unroll=2)
+    lax.fori_loop(0, units, halo_unit, 0, unroll=units)
     tang_out = pltpu.make_async_copy(tang, tang_h, out_sem.at[1])
     tang_out.start()
 
@@ -405,7 +448,10 @@
             pltpu.VMEM((levels, edges), jnp.float32),
             pltpu.VMEM((levels, edges), jnp.float32),
             exchange, exchange, exchange, exchange,
-            pltpu.VMEM((units, (group + 1) * 3 * levels, SUB, LANES), jnp.float32),
+            pltpu.VMEM((units, (group + 1) * 2 * levels, SUB, LANES), jnp.float32),
+            pltpu.VMEM((units, (group + 1) * (levels // 2), SUB, LANES), jnp.int32),
+            pltpu.VMEM((levels // 2, edges), jnp.int32),
+            pltpu.VMEM((SUB * blocks, LANES), jnp.int32),
             pltpu.VMEM((cells // LANES * levels, SUB, LANES), jnp.float32),
             pltpu.VMEM((SUB, LANES), jnp.int32),
             dma(len(args)), dma(blocks), dma(blocks), dma(blocks), dma(blocks), dma(2), dma(2), dma(3),

time: 18.3 us -> 17.9 us (0.978)
  Pallas kernels: 17.4 us -> 17.1 us
    pallas_call x1, Pallas kernels: 16 us -> 15.6 us  [body(): pl.pallas_call(functools.partial(kernel, lax.axis_size('mesh'), lax.axis_...]
where the time goes in v5:
time: 17.9 us; the launch traced here: 17.7 us
  Pallas kernels  17.1 us (96%)
  between operations  0.64 us (4%)
    pallas_call x1, Pallas kernels, body(): pl.pallas_call(functools.partial(kernel, lax.axis_size('mesh'), lax.axis_...  15.6 us
    pallas_call x1, Pallas kernels, body(): pl.pallas_call(place, out_shape=results, in_specs=[anywhere] * 3, out_spe...  1.42 us

profile of v5, /device:TPU:0, one launch (start us, length us, event | category | flops | bytes accessed | tf_op | source)
XLA Modules:
  0.0 17.7 jit_solution(5875813038118509055)
XLA Ops:
  0.6 15.6 %shard_map.157 = (f32[2,3072]{1,0:T(2,128)}, f32[2,3072]{1,0:T(2,128)}, f32[2,1024]{1,0:T(2,128)}) custom-call(f32[2,3072]{1,0:T(2,128)} %vel_h.1, f32[2,3072]{1,0:T(2,128)} %thk_h.1, f32[2,3072]{1,0:T(2,128)} %vor_h.1, f32[2,3072]{1,0:T(2,128)} %wind_h.1, f32[10,3072]{1,0:T(8,128)} %wts_h.1, s32[10,3072]{1,0:T(8,128)} %eoe_h.1, s32[6,1024]{1,0:T(8,128)} %eoc_h.1, ...), custom_call_target="tpu_custom_call" | custom-call | tf_op jit(solution)/shard_map/pallas_call | solution.py:438
  16.3 1.4 %shard_map.158 = (f32[2,3072]{1,0:T(2,128)}, f32[2,3072]{1,0:T(2,128)}, f32[2,1024]{1,0:T(2,128)}) custom-call(f32[2,3072]{1,0:T(2,128)} %get-tuple-element.6.refs_0_, f32[2,3072]{1,0:T(2,128)} %get-tuple-element.7.refs_1_, f32[2,1024]{1,0:T(2,128)} %get-tuple-element.8.refs_2_), custom_call_target="tpu_custom_call" | custom-call | tf_op jit(solution)/shard_map/pallas_call | solution.py:461

commit v6 on v5

--- a/solution.py
+++ b/solution.py
@@ -158,6 +158,38 @@
         for o in range(blocks):
             esend[SUB * o + p : SUB * o + p + 1, :] = block[o : o + 1]
 
+    for i in range(pairs_of):
+        code[i : i + 1, :] = coded(thk[2 * i : 2 * i + 1, :], thk[2 * i + 1 : 2 * i + 2, :])
+
+    loads[6].wait()
+
+    def unit_lookups(u):
+        lookups = []
+        for q in range(group):
+            index = eoe[0:SUB, tile(u * group + q)]
+            lookups.append((index >> 7, index & 127))
+        index = jnp.concatenate(
+            [eoe[SUB:neoe, tile(u * group + q)] for q in range(group)], axis=0
+        )
+        lookups.append((index >> 7, index & 127))
+        return lookups
+
+    none = (blank,) * exact + (jnp.zeros((SUB, LANES), jnp.int32),) * pairs_of
+
+    def local_unit(u, carry):
+        found = scan(
+            0, edge_rows, table_rows, unit_lookups(u), [none] * (group + 1), edge_rows
+        )
+        for g in range(group + 1):
+            for p in range(exact):
+                near[u, g * exact + p] = found[g][p]
+            for i in range(pairs_of):
+                near_code[u, g * pairs_of + i] = found[g][exact + i]
+        return carry
+
+    early, middle = units // 3, 2 * units // 3
+    lax.fori_loop(0, early, local_unit, 0, unroll=2)
+
     pl.semaphore_wait(barrier, blocks + 2)
     edge_copies = []
     for o in range(blocks):
@@ -185,9 +217,6 @@
         copy.start()
         rim_copies.append(copy)
 
-    for i in range(pairs_of):
-        code[i : i + 1, :] = coded(thk[2 * i : 2 * i + 1, :], thk[2 * i + 1 : 2 * i + 2, :])
-
     loads[5].wait()
     cell_lookups = []
     for c in range(cell_rows):
@@ -200,33 +229,7 @@
         for l in range(levels):
             cell_near[c * levels + l] = found[c][l]
 
-    loads[6].wait()
-
-    def unit_lookups(u):
-        lookups = []
-        for q in range(group):
-            index = eoe[0:SUB, tile(u * group + q)]
-            lookups.append((index >> 7, index & 127))
-        index = jnp.concatenate(
-            [eoe[SUB:neoe, tile(u * group + q)] for q in range(group)], axis=0
-        )
-        lookups.append((index >> 7, index & 127))
-        return lookups
-
-    none = (blank,) * exact + (jnp.zeros((SUB, LANES), jnp.int32),) * pairs_of
-
-    def local_unit(u, carry):
-        found = scan(
-            0, edge_rows, table_rows, unit_lookups(u), [none] * (group + 1), edge_rows
-        )
-        for g in range(group + 1):
-            for p in range(exact):
-                near[u, g * exact + p] = found[g][p]
-            for i in range(pairs_of):
-                near_code[u, g * pairs_of + i] = found[g][exact + i]
-        return carry
-
-    lax.fori_loop(0, units, local_unit, 0, unroll=2)
+    lax.fori_loop(early, middle, local_unit, 0, unroll=2)
 
     for copy in edge_copies:
         copy.wait()
@@ -293,6 +296,8 @@
         )
         copy.start()
         cell_copies.append(copy)
+
+    lax.fori_loop(middle, units, local_unit, 0, unroll=2)
 
     loads[8].wait()
 
@@ -336,47 +341,54 @@
     tang_out = pltpu.make_async_copy(tang, tang_h, out_sem.at[1])
     tang_out.start()
 
-    for copy in cell_copies + rim_copies + loads[11:]:
+    for copy in rim_copies + loads[11:]:
         copy.wait()
     ends = SUB // 2
-
-    def end_unit(u, carry):
-        cols = [tile(u * ends + q) for q in range(ends)]
-        index = jnp.concatenate([coe[:, c] for c in cols], axis=0)
+    end_units = edge_rows // ends
+    places = []
+    for u in range(end_units):
+        index = jnp.concatenate([coe[:, tile(u * ends + q)] for q in range(ends)], axis=0)
         far = index >= cells
         slot = index - cells
-        place = (
+        places.append((
             jnp.where(far, cell_rows + slot // halo_c, index >> 7),
             jnp.where(far, slot % halo_c, index & 127),
-        )
-
-        def received_rows(k):
-            start = pl.multiple_of(SUB * (k - cell_rows), SUB)
-            rows = crecv[pl.ds(start, SUB), :]
-            return [spread(rows[l : l + 1]) for l in range(levels)]
-
-        found = scan(0, cell_rows, energy_rows, [place], [(blank,) * levels], cell_rows)
-        (found,) = scan(cell_rows, cell_rows + blocks, received_rows, [place], found, blocks)
-        for q, c in enumerate(cols):
-            rows = []
-            for l in range(levels):
-                gradient = (
-                    found[l][2 * q + 1 : 2 * q + 2] - found[l][2 * q : 2 * q + 1]
-                ) * invd[pl.ds(u * ends + q, 1), :]
-                if l + 1 < levels:
-                    over = vel[l + 1 : l + 2, c]
-                else:
-                    over = jnp.where(lev == n_lev - 1, 0.0, above[0:1, c])
-                if l > 0:
-                    under = vel[l - 1 : l, c]
-                else:
-                    under = jnp.where(lev == 0, 0.0, below[levels - 1 : levels, c])
-                advect = -0.5 * wind[l : l + 1, c] * (over - under)
-                rows.append((tend[l : l + 1, c] - gradient) + advect)
-            tend[:, c] = jnp.concatenate(rows, axis=0)
-        return carry
-
-    lax.fori_loop(0, edge_rows // ends, end_unit, 0, unroll=edge_rows // ends)
+        ))
+    found = scan(
+        0, cell_rows, energy_rows, places, [(blank,) * levels] * end_units, cell_rows
+    )
+    for c in range(edge_rows):
+        col = tile(c)
+        for l in range(levels):
+            if l + 1 < levels:
+                over = vel[l + 1 : l + 2, col]
+            else:
+                over = jnp.where(lev == n_lev - 1, 0.0, above[0:1, col])
+            if l > 0:
+                under = vel[l - 1 : l, col]
+            else:
+                under = jnp.where(lev == 0, 0.0, below[levels - 1 : levels, col])
+            wind[l : l + 1, col] = -0.5 * wind[l : l + 1, col] * (over - under)
+
+    def received_rows(k):
+        start = pl.multiple_of(SUB * (k - cell_rows), SUB)
+        rows = crecv[pl.ds(start, SUB), :]
+        return [spread(rows[l : l + 1]) for l in range(levels)]
+
+    for copy in cell_copies:
+        copy.wait()
+    found = scan(cell_rows, cell_rows + blocks, received_rows, places, found, blocks)
+    for c in range(edge_rows):
+        u, q = c // ends, c % ends
+        gradient = jnp.concatenate(
+            [
+                found[u][l][2 * q + 1 : 2 * q + 2] - found[u][l][2 * q : 2 * q + 1]
+                for l in range(levels)
+            ],
+            axis=0,
+        ) * invd[c : c + 1, :]
+        tend[:, tile(c)] = (tend[:, tile(c)] - gradient) + wind[:, tile(c)]
+
     tend_out = pltpu.make_async_copy(tend, tend_h, out_sem.at[2])
     tend_out.start()
     for copy in (energy_out, tang_out, tend_out):

time: 17.9 us -> 17.8 us (level)
  no operation moved by 1% of the time
where the time goes in v6:
time: 17.8 us; the launch traced here: 17.6 us
  Pallas kernels  17 us (96%)
  between operations  0.64 us (4%)
    pallas_call x1, Pallas kernels, body(): pl.pallas_call(functools.partial(kernel, lax.axis_size('mesh'), lax.axis_...  15.5 us
    pallas_call x1, Pallas kernels, body(): pl.pallas_call(place, out_shape=results, in_specs=[anywhere] * 3, out_spe...  1.42 us

profile of v6, /device:TPU:0, one launch (start us, length us, event | category | flops | bytes accessed | tf_op | source)
XLA Modules:
  0.0 17.6 jit_solution(10046979077248247776)
XLA Ops:
  0.6 15.5 %shard_map.157 = (f32[2,3072]{1,0:T(2,128)}, f32[2,3072]{1,0:T(2,128)}, f32[2,1024]{1,0:T(2,128)}) custom-call(f32[2,3072]{1,0:T(2,128)} %vel_h.1, f32[2,3072]{1,0:T(2,128)} %thk_h.1, f32[2,3072]{1,0:T(2,128)} %vor_h.1, f32[2,3072]{1,0:T(2,128)} %wind_h.1, f32[10,3072]{1,0:T(8,128)} %wts_h.1, s32[10,3072]{1,0:T(8,128)} %eoe_h.1, s32[6,1024]{1,0:T(8,128)} %eoc_h.1, ...), custom_call_target="tpu_custom_call" | custom-call | tf_op jit(solution)/shard_map/pallas_call | solution.py:450
  16.2 1.4 %shard_map.158 = (f32[2,3072]{1,0:T(2,128)}, f32[2,3072]{1,0:T(2,128)}, f32[2,1024]{1,0:T(2,128)}) custom-call(f32[2,3072]{1,0:T(2,128)} %get-tuple-element.6.refs_0_, f32[2,3072]{1,0:T(2,128)} %get-tuple-element.7.refs_1_, f32[2,1024]{1,0:T(2,128)} %get-tuple-element.8.refs_2_), custom_call_target="tpu_custom_call" | custom-call | tf_op jit(solution)/shard_map/pallas_call | solution.py:473

commit v7 on v6

--- a/solution.py
+++ b/solution.py
@@ -74,7 +74,7 @@
     vel_h, thk_h, vor_h, wind_h, wts_h, eoe_h, eoc_h, coe_h, ew_h, invd_h, ehl_h, ehc_h, chl_h, chc_h,
     tend_h, tang_h, energy_h,
     vel, thk, vor, wind, wts, eoe, eoc, coe, ew, invd, ehl, ehc, chl, chc,
-    tend, tang, energy, below, above, esend, erecv, csend, crecv, near, near_code, code, code_halo, cell_near, cell_pick,
+    tend, tang, energy, below, above, esend, erecv, csend, crecv, near, near_code, code, code_halo, cell_pick,
     load_sem, es_sem, er_sem, cs_sem, cr_sem, ls_sem, lr_sem, out_sem,
 ):
     levels, edges = vel.shape
@@ -146,6 +146,32 @@
     def padded_rows(x):
         return jnp.concatenate([x, jnp.zeros((SUB - x.shape[0], LANES), x.dtype)], axis=0)
 
+    def halo_copy(source, target, sent, arrived, o):
+        rows = pl.ds(SUB * o, SUB)
+        return pltpu.make_async_remote_copy(
+            src_ref=source.at[rows],
+            dst_ref=target.at[rows],
+            send_sem=sent.at[o],
+            recv_sem=arrived.at[o],
+            device_id=partner(o),
+            device_id_type=MESH,
+        )
+
+    edge_copies = [halo_copy(esend, erecv, es_sem, er_sem, o) for o in range(blocks)]
+    cell_copies = [halo_copy(csend, crecv, cs_sem, cr_sem, o) for o in range(blocks)]
+    rim_copies = [
+        pltpu.make_async_remote_copy(
+            src_ref=vel,
+            dst_ref=dst,
+            send_sem=ls_sem.at[i],
+            recv_sem=lr_sem.at[i],
+            device_id=target,
+            device_id_type=MESH,
+        )
+        for i, (dst, target) in enumerate(((below, up), (above, down)))
+    ]
+    energy_out = pltpu.make_async_copy(energy, energy_h, out_sem.at[0])
+
     for copy in loads[:5]:
         copy.wait()
     index = padded_rows(ehl[...])
@@ -186,61 +212,6 @@
             for i in range(pairs_of):
                 near_code[u, g * pairs_of + i] = found[g][exact + i]
         return carry
-
-    early, middle = units // 3, 2 * units // 3
-    lax.fori_loop(0, early, local_unit, 0, unroll=2)
-
-    pl.semaphore_wait(barrier, blocks + 2)
-    edge_copies = []
-    for o in range(blocks):
-        rows = pl.ds(SUB * o, SUB)
-        copy = pltpu.make_async_remote_copy(
-            src_ref=esend.at[rows],
-            dst_ref=erecv.at[rows],
-            send_sem=es_sem.at[o],
-            recv_sem=er_sem.at[o],
-            device_id=partner(o),
-            device_id_type=MESH,
-        )
-        copy.start()
-        edge_copies.append(copy)
-    rim_copies = []
-    for i, (dst, target) in enumerate(((below, up), (above, down))):
-        copy = pltpu.make_async_remote_copy(
-            src_ref=vel,
-            dst_ref=dst,
-            send_sem=ls_sem.at[i],
-            recv_sem=lr_sem.at[i],
-            device_id=target,
-            device_id_type=MESH,
-        )
-        copy.start()
-        rim_copies.append(copy)
-
-    loads[5].wait()
-    cell_lookups = []
-    for c in range(cell_rows):
-        index = padded_rows(eoc[:, c * LANES : (c + 1) * LANES])
-        cell_lookups.append((index >> 7, index & 127))
-    found = scan(
-        0, edge_rows, speed_rows, cell_lookups, [(blank,) * levels] * cell_rows, edge_rows
-    )
-    for c in range(cell_rows):
-        for l in range(levels):
-            cell_near[c * levels + l] = found[c][l]
-
-    lax.fori_loop(early, middle, local_unit, 0, unroll=2)
-
-    for copy in edge_copies:
-        copy.wait()
-    loads[7].wait()
-
-    for o in range(blocks):
-        for i in range(pairs_of):
-            first = SUB * o + levels + 2 * i
-            code_halo[SUB * o + i : SUB * o + i + 1, :] = coded(
-                erecv[first : first + 1, :], erecv[first + 1 : first + 2, :]
-            )
 
     def halo_rows(which, codes):
         def load(k):
@@ -254,50 +225,65 @@
 
         return load
 
-    found = [
-        tuple(cell_near[c * levels + l] for l in range(levels)) for c in range(cell_rows)
-    ]
-    found = scan(edge_rows, edge_rows + blocks, halo_rows(range(levels), False), cell_lookups, found, blocks)
-    for c in range(cell_rows):
-        weight = padded_rows(ew[:, c * LANES : (c + 1) * LANES])
-        energy[:, c * LANES : (c + 1) * LANES] = jnp.concatenate(
-            [total_rows(weight * found[c][l] * found[c][l]) for l in range(levels)], axis=0
-        )
-
-    energy_out = pltpu.make_async_copy(energy, energy_h, out_sem.at[0])
-    energy_out.start()
-
-    for copy in loads[9:11]:
-        copy.wait()
-    cell_pick[0:blocks, 0:halo_c] = chl[...]
-    index = cell_pick[...]
-
     def energy_rows(k):
         return [spread(energy[l : l + 1, tile(k)]) for l in range(levels)]
 
-    (packed,) = scan(
-        0, cell_rows, energy_rows, [(index >> 7, index & 127)], [(blank,) * levels], cell_rows
-    )
-    alive = live(chc)
-    for l in range(levels):
-        block = jnp.where(alive, packed[l], 0.0)
+    def edges_leave():
+        pl.semaphore_wait(barrier, blocks + 2)
+        for copy in edge_copies + rim_copies:
+            copy.start()
+
+    def energy_step():
+        loads[5].wait()
+        cell_lookups = []
+        for c in range(cell_rows):
+            index = padded_rows(eoc[:, c * LANES : (c + 1) * LANES])
+            cell_lookups.append((index >> 7, index & 127))
+        found = scan(
+            0, edge_rows, speed_rows, cell_lookups, [(blank,) * levels] * cell_rows, edge_rows
+        )
+        for copy in edge_copies:
+            copy.wait()
+        loads[7].wait()
+
         for o in range(blocks):
-            csend[SUB * o + l : SUB * o + l + 1, :] = block[o : o + 1]
-    cell_copies = []
-    for o in range(blocks):
-        rows = pl.ds(SUB * o, SUB)
-        copy = pltpu.make_async_remote_copy(
-            src_ref=csend.at[rows],
-            dst_ref=crecv.at[rows],
-            send_sem=cs_sem.at[o],
-            recv_sem=cr_sem.at[o],
-            device_id=partner(o),
-            device_id_type=MESH,
-        )
-        copy.start()
-        cell_copies.append(copy)
-
-    lax.fori_loop(middle, units, local_unit, 0, unroll=2)
+            for i in range(pairs_of):
+                first = SUB * o + levels + 2 * i
+                code_halo[SUB * o + i : SUB * o + i + 1, :] = coded(
+                    erecv[first : first + 1, :], erecv[first + 1 : first + 2, :]
+                )
+
+        found = scan(edge_rows, edge_rows + blocks, halo_rows(range(levels), False), cell_lookups, found, blocks)
+        for c in range(cell_rows):
+            weight = padded_rows(ew[:, c * LANES : (c + 1) * LANES])
+            energy[:, c * LANES : (c + 1) * LANES] = jnp.concatenate(
+                [total_rows(weight * found[c][l] * found[c][l]) for l in range(levels)], axis=0
+            )
+
+        energy_out.start()
+
+        for copy in loads[9:11]:
+            copy.wait()
+        cell_pick[0:blocks, 0:halo_c] = chl[...]
+        index = cell_pick[...]
+
+        (packed,) = scan(
+            0, cell_rows, energy_rows, [(index >> 7, index & 127)], [(blank,) * levels], cell_rows
+        )
+        alive = live(chc)
+        for l in range(levels):
+            block = jnp.where(alive, packed[l], 0.0)
+            for o in range(blocks):
+                csend[SUB * o + l : SUB * o + l + 1, :] = block[o : o + 1]
+        for copy in cell_copies:
+            copy.start()
+
+    def unit_step(u, carry):
+        pl.when(u == units // 3)(edges_leave)
+        pl.when(u == 2 * units // 3)(energy_step)
+        return local_unit(u, carry)
+
+    lax.fori_loop(0, units, unit_step, 0)
 
     loads[8].wait()
 
@@ -337,7 +323,7 @@
             tend[:, c] = jnp.concatenate(fluxes[q], axis=0)
         return carry
 
-    lax.fori_loop(0, units, halo_unit, 0, unroll=units)
+    lax.fori_loop(0, units, halo_unit, 0, unroll=2)
     tang_out = pltpu.make_async_copy(tang, tang_h, out_sem.at[1])
     tang_out.start()
 
@@ -464,7 +450,6 @@
             pltpu.VMEM((units, (group + 1) * (levels // 2), SUB, LANES), jnp.int32),
             pltpu.VMEM((levels // 2, edges), jnp.int32),
             pltpu.VMEM((SUB * blocks, LANES), jnp.int32),
-            pltpu.VMEM((cells // LANES * levels, SUB, LANES), jnp.float32),
             pltpu.VMEM((SUB, LANES), jnp.int32),
             dma(len(args)), dma(blocks), dma(blocks), dma(blocks), dma(blocks), dma(2), dma(2), dma(3),
         ],

time: 17.8 us -> 17.8 us (level)
  no operation moved by 1% of the time
where the time goes in v7:
time: 17.8 us; the launch traced here: 17.6 us
  Pallas kernels  17 us (96%)
  between operations  0.64 us (4%)
    pallas_call x1, Pallas kernels, body(): pl.pallas_call(functools.partial(kernel, lax.axis_size('mesh'), lax.axis_...  15.5 us
    pallas_call x1, Pallas kernels, body(): pl.pallas_call(place, out_shape=results, in_specs=[anywhere] * 3, out_spe...  1.42 us

profile of v7, /device:TPU:0, one launch (start us, length us, event | category | flops | bytes accessed | tf_op | source)
XLA Modules:
  0.0 17.6 jit_solution(4750289406229834453)
XLA Ops:
  0.6 15.5 %shard_map.157 = (f32[2,3072]{1,0:T(2,128)}, f32[2,3072]{1,0:T(2,128)}, f32[2,1024]{1,0:T(2,128)}) custom-call(f32[2,3072]{1,0:T(2,128)} %vel_h.1, f32[2,3072]{1,0:T(2,128)} %thk_h.1, f32[2,3072]{1,0:T(2,128)} %vor_h.1, f32[2,3072]{1,0:T(2,128)} %wind_h.1, f32[10,3072]{1,0:T(8,128)} %wts_h.1, s32[10,3072]{1,0:T(8,128)} %eoe_h.1, s32[6,1024]{1,0:T(8,128)} %eoc_h.1, ...), custom_call_target="tpu_custom_call" | custom-call | tf_op jit(solution)/shard_map/pallas_call | solution.py:436
  16.2 1.4 %shard_map.158 = (f32[2,3072]{1,0:T(2,128)}, f32[2,3072]{1,0:T(2,128)}, f32[2,1024]{1,0:T(2,128)}) custom-call(f32[2,3072]{1,0:T(2,128)} %get-tuple-element.6.refs_0_, f32[2,3072]{1,0:T(2,128)} %get-tuple-element.7.refs_1_, f32[2,1024]{1,0:T(2,128)} %get-tuple-element.8.refs_2_), custom_call_target="tpu_custom_call" | custom-call | tf_op jit(solution)/shard_map/pallas_call | solution.py:458

commit v8 on v7

--- a/solution.py
+++ b/solution.py
@@ -184,10 +184,6 @@
         for o in range(blocks):
             esend[SUB * o + p : SUB * o + p + 1, :] = block[o : o + 1]
 
-    for i in range(pairs_of):
-        code[i : i + 1, :] = coded(thk[2 * i : 2 * i + 1, :], thk[2 * i + 1 : 2 * i + 2, :])
-
-    loads[6].wait()
 
     def unit_lookups(u):
         lookups = []
@@ -279,10 +275,13 @@
             copy.start()
 
     def unit_step(u, carry):
-        pl.when(u == units // 3)(edges_leave)
         pl.when(u == 2 * units // 3)(energy_step)
         return local_unit(u, carry)
 
+    edges_leave()
+    for i in range(pairs_of):
+        code[i : i + 1, :] = coded(thk[2 * i : 2 * i + 1, :], thk[2 * i + 1 : 2 * i + 2, :])
+    loads[6].wait()
     lax.fori_loop(0, units, unit_step, 0)
 
     loads[8].wait()

time: 17.8 us -> 17.8 us (level)
  no operation moved by 1% of the time
where the time goes in v8:
time: 17.8 us; the launch traced here: 17.6 us
  Pallas kernels  17 us (96%)
  between operations  0.64 us (4%)
    pallas_call x1, Pallas kernels, body(): pl.pallas_call(functools.partial(kernel, lax.axis_size('mesh'), lax.axis_...  15.5 us
    pallas_call x1, Pallas kernels, body(): pl.pallas_call(place, out_shape=results, in_specs=[anywhere] * 3, out_spe...  1.42 us

profile of v8, /device:TPU:0, one launch (start us, length us, event | category | flops | bytes accessed | tf_op | source)
XLA Modules:
  0.0 17.6 jit_solution(17844810841673109822)
XLA Ops:
  0.6 15.5 %shard_map.157 = (f32[2,3072]{1,0:T(2,128)}, f32[2,3072]{1,0:T(2,128)}, f32[2,1024]{1,0:T(2,128)}) custom-call(f32[2,3072]{1,0:T(2,128)} %vel_h.1, f32[2,3072]{1,0:T(2,128)} %thk_h.1, f32[2,3072]{1,0:T(2,128)} %vor_h.1, f32[2,3072]{1,0:T(2,128)} %wind_h.1, f32[10,3072]{1,0:T(8,128)} %wts_h.1, s32[10,3072]{1,0:T(8,128)} %eoe_h.1, s32[6,1024]{1,0:T(8,128)} %eoc_h.1, ...), custom_call_target="tpu_custom_call" | custom-call | tf_op jit(solution)/shard_map/pallas_call | solution.py:435
  16.2 1.4 %shard_map.158 = (f32[2,3072]{1,0:T(2,128)}, f32[2,3072]{1,0:T(2,128)}, f32[2,1024]{1,0:T(2,128)}) custom-call(f32[2,3072]{1,0:T(2,128)} %get-tuple-element.6.refs_0_, f32[2,3072]{1,0:T(2,128)} %get-tuple-element.7.refs_1_, f32[2,1024]{1,0:T(2,128)} %get-tuple-element.8.refs_2_), custom_call_target="tpu_custom_call" | custom-call | tf_op jit(solution)/shard_map/pallas_call | solution.py:457

commit v9 on v8

--- a/solution.py
+++ b/solution.py
@@ -71,10 +71,10 @@
 def kernel(
     n_mesh,
     n_lev,
-    vel_h, thk_h, vor_h, wind_h, wts_h, eoe_h, eoc_h, coe_h, ew_h, invd_h, ehl_h, ehc_h, chl_h, chc_h,
-    tend_h, tang_h, energy_h,
-    vel, thk, vor, wind, wts, eoe, eoc, coe, ew, invd, ehl, ehc, chl, chc,
-    tend, tang, energy, below, above, esend, erecv, csend, crecv, near, near_code, code, code_halo, cell_pick,
+    vel_h, thk_h, vor_h, wind_h, wts_h, eoe_h, eoc_h, ew_h, ehl_h, ehc_h, chl_h, chc_h,
+    tend_h, tang_h, energy_h, crecv,
+    vel, thk, vor, wind, wts, eoe, eoc, ew, ehl, ehc, chl, chc,
+    tend, tang, energy, below, above, esend, erecv, csend, near, near_code, code, code_halo, cell_pick,
     load_sem, es_sem, er_sem, cs_sem, cr_sem, ls_sem, lr_sem, out_sem,
 ):
     levels, edges = vel.shape
@@ -94,6 +94,8 @@
     me = lax.axis_index("mesh")
     lev = lax.axis_index("lev")
 
+    order = sorted(range(blocks), key=lambda o: o % reach)
+
     def partner(o):
         offset = o + 1 if o < reach else reach - 1 - o
         return {"mesh": lax.rem(me + offset + n_mesh, n_mesh)}
@@ -102,7 +104,7 @@
     down = {"lev": lax.rem(lev + n_lev - 1, n_lev)}
 
     barrier = pltpu.get_barrier_semaphore()
-    for o in range(blocks):
+    for o in order:
         pl.semaphore_signal(barrier, inc=1, device_id=partner(o), device_id_type=MESH)
     pl.semaphore_signal(barrier, inc=1, device_id=up, device_id_type=MESH)
     pl.semaphore_signal(barrier, inc=1, device_id=down, device_id_type=MESH)
@@ -110,7 +112,7 @@
     pairs = [
         (ehl_h, ehl), (ehc_h, ehc), (vel_h, vel), (thk_h, thk), (vor_h, vor),
         (eoc_h, eoc), (eoe_h, eoe), (ew_h, ew), (wts_h, wts), (chl_h, chl), (chc_h, chc),
-        (coe_h, coe), (invd_h, invd), (wind_h, wind),
+        (wind_h, wind),
     ]
     loads = []
     for i, (src, dst) in enumerate(pairs):
@@ -157,8 +159,8 @@
             device_id_type=MESH,
         )
 
-    edge_copies = [halo_copy(esend, erecv, es_sem, er_sem, o) for o in range(blocks)]
-    cell_copies = [halo_copy(csend, crecv, cs_sem, cr_sem, o) for o in range(blocks)]
+    edge_copies = [halo_copy(esend, erecv, es_sem, er_sem, o) for o in order]
+    cell_copies = [halo_copy(csend, crecv, cs_sem, cr_sem, o) for o in order]
     rim_copies = [
         pltpu.make_async_remote_copy(
             src_ref=vel,
@@ -275,10 +277,10 @@
             copy.start()
 
     def unit_step(u, carry):
+        pl.when(u == units // 6)(edges_leave)
         pl.when(u == 2 * units // 3)(energy_step)
         return local_unit(u, carry)
 
-    edges_leave()
     for i in range(pairs_of):
         code[i : i + 1, :] = coded(thk[2 * i : 2 * i + 1, :], thk[2 * i + 1 : 2 * i + 2, :])
     loads[6].wait()
@@ -328,20 +330,6 @@
 
     for copy in rim_copies + loads[11:]:
         copy.wait()
-    ends = SUB // 2
-    end_units = edge_rows // ends
-    places = []
-    for u in range(end_units):
-        index = jnp.concatenate([coe[:, tile(u * ends + q)] for q in range(ends)], axis=0)
-        far = index >= cells
-        slot = index - cells
-        places.append((
-            jnp.where(far, cell_rows + slot // halo_c, index >> 7),
-            jnp.where(far, slot % halo_c, index & 127),
-        ))
-    found = scan(
-        0, cell_rows, energy_rows, places, [(blank,) * levels] * end_units, cell_rows
-    )
     for c in range(edge_rows):
         col = tile(c)
         for l in range(levels):
@@ -354,14 +342,65 @@
             else:
                 under = jnp.where(lev == 0, 0.0, below[levels - 1 : levels, col])
             wind[l : l + 1, col] = -0.5 * wind[l : l + 1, col] * (over - under)
+    tend[...] = tend[...] + wind[...]
+
+    tend_out = pltpu.make_async_copy(tend, tend_h, out_sem.at[2])
+    tend_out.start()
+    for copy in (energy_out, tang_out, tend_out):
+        copy.wait()
+    for copy in cell_copies:
+        copy.wait()
+
+
+def finish(
+    halo_c,
+    crecv_h, energy_h, coe_h, invd_h, tend_h, tang_h,
+    tend_o, tang_o, energy_o,
+    crecv, energy, coe, invd, tend, tang, in_sem, out_sem,
+):
+    levels, cells = energy.shape
+    edge_rows, cell_rows = invd.shape[0], cells // LANES
+    blocks = crecv.shape[0] // SUB
+    sources = (crecv_h, energy_h, coe_h, invd_h, tend_h, tang_h)
+    held = (crecv, energy, coe, invd, tend, tang)
+    ins = [
+        pltpu.make_async_copy(a, b, in_sem.at[i]) for i, (a, b) in enumerate(zip(sources, held))
+    ]
+    for copy in ins:
+        copy.start()
+    outs = [
+        pltpu.make_async_copy(a, b, out_sem.at[i])
+        for i, (a, b) in enumerate(((energy, energy_o), (tang, tang_o), (tend, tend_o)))
+    ]
+    for copy in ins:
+        copy.wait()
+    outs[0].start()
+    outs[1].start()
+
+    blank = jnp.zeros((SUB, LANES), jnp.float32)
+    ends = SUB // 2
+    end_units = edge_rows // ends
+    places = []
+    for u in range(end_units):
+        index = jnp.concatenate([coe[:, tile(u * ends + q)] for q in range(ends)], axis=0)
+        far = index >= cells
+        slot = index - cells
+        places.append((
+            jnp.where(far, cell_rows + slot // halo_c, index >> 7),
+            jnp.where(far, slot % halo_c, index & 127),
+        ))
+
+    def energy_rows(k):
+        return [spread(energy[l : l + 1, tile(k)]) for l in range(levels)]
 
     def received_rows(k):
         start = pl.multiple_of(SUB * (k - cell_rows), SUB)
         rows = crecv[pl.ds(start, SUB), :]
         return [spread(rows[l : l + 1]) for l in range(levels)]
 
-    for copy in cell_copies:
-        copy.wait()
+    found = scan(
+        0, cell_rows, energy_rows, places, [(blank,) * levels] * end_units, cell_rows
+    )
     found = scan(cell_rows, cell_rows + blocks, received_rows, places, found, blocks)
     for c in range(edge_rows):
         u, q = c // ends, c % ends
@@ -372,25 +411,8 @@
             ],
             axis=0,
         ) * invd[c : c + 1, :]
-        tend[:, tile(c)] = (tend[:, tile(c)] - gradient) + wind[:, tile(c)]
-
-    tend_out = pltpu.make_async_copy(tend, tend_h, out_sem.at[2])
-    tend_out.start()
-    for copy in (energy_out, tang_out, tend_out):
-        copy.wait()
-
-
-def place(*refs):
-    *arrays, in_sem, out_sem = refs
-    count = len(arrays) // 3
-    sources, targets, held = (arrays[i * count : (i + 1) * count] for i in range(3))
-    ins = [pltpu.make_async_copy(sources[i], held[i], in_sem.at[i]) for i in range(count)]
-    outs = [pltpu.make_async_copy(held[i], targets[i], out_sem.at[i]) for i in range(count)]
-    for copy in ins:
-        copy.start()
-    for arrived, leaving in zip(ins, outs):
-        arrived.wait()
-        leaving.start()
+        tend[:, tile(c)] = tend[:, tile(c)] - gradient
+    outs[2].start()
     for copy in outs:
         copy.wait()
 
@@ -418,13 +440,13 @@
     units = edges // (LANES * group)
     args = [
         velocity, thickness, vorticity, vertical_wind, weights_on_edge, edges_on_edge,
-        edges_on_cell, cells_on_edge, energy_weight, inverse_distance.reshape(-1, LANES),
-        edge_halo_list, edge_halo_count, cell_halo_list, cell_halo_count,
+        edges_on_cell, energy_weight, edge_halo_list, edge_halo_count, cell_halo_list, cell_halo_count,
     ]
     held = [
         pltpu.SMEM(a.shape, a.dtype) if a.ndim == 1 else pltpu.VMEM(a.shape, a.dtype) for a in args
     ]
     exchange = pltpu.VMEM((SUB * blocks, LANES), jnp.float32)
+    landed = jax.ShapeDtypeStruct((SUB * blocks, LANES), jnp.float32)
     dma = lambda n: pltpu.SemaphoreType.DMA((n,))
     results = (
         jax.ShapeDtypeStruct((levels, edges), jnp.float32),
@@ -432,11 +454,11 @@
         jax.ShapeDtypeStruct((levels, cells), jnp.float32),
     )
     anywhere = pl.BlockSpec(memory_space=pl.ANY)
-    found = pl.pallas_call(
+    partial, tangent, energy, cell_halo = pl.pallas_call(
         functools.partial(kernel, lax.axis_size("mesh"), lax.axis_size("lev")),
-        out_shape=results,
+        out_shape=results + (landed,),
         in_specs=[anywhere] * len(args),
-        out_specs=(anywhere,) * 3,
+        out_specs=(anywhere,) * 4,
         scratch_shapes=held
         + [
             pltpu.VMEM((levels, edges), jnp.float32),
@@ -444,7 +466,7 @@
             pltpu.VMEM((levels, cells), jnp.float32),
             pltpu.VMEM((levels, edges), jnp.float32),
             pltpu.VMEM((levels, edges), jnp.float32),
-            exchange, exchange, exchange, exchange,
+            exchange, exchange, exchange,
             pltpu.VMEM((units, (group + 1) * 2 * levels, SUB, LANES), jnp.float32),
             pltpu.VMEM((units, (group + 1) * (levels // 2), SUB, LANES), jnp.int32),
             pltpu.VMEM((levels // 2, edges), jnp.int32),
@@ -454,13 +476,16 @@
         ],
         compiler_params=pltpu.CompilerParams(collective_id=0, has_side_effects=True),
     )(*args)
+    rest = (
+        cell_halo, energy, cells_on_edge, inverse_distance.reshape(-1, LANES), partial, tangent
+    )
     return pl.pallas_call(
-        place,
+        functools.partial(finish, cell_halo_list.shape[1]),
         out_shape=results,
-        in_specs=[anywhere] * 3,
+        in_specs=[anywhere] * len(rest),
         out_specs=(anywhere,) * 3,
-        scratch_shapes=[pltpu.VMEM(r.shape, r.dtype) for r in results] + [dma(3), dma(3)],
-    )(*found)
+        scratch_shapes=[pltpu.VMEM(a.shape, a.dtype) for a in rest] + [dma(len(rest)), dma(3)],
+    )(*rest)
 
 
 def solution(mesh):

time: 17.8 us -> 17.4 us (0.978)
  Pallas kernels: 17 us -> 16.6 us
    pallas_call x1, Pallas kernels: 15.5 us -> 14.8 us  [body(): pl.pallas_call(functools.partial(kernel, lax.axis_size('mesh'), lax.axis_...]
    pallas_call x1, Pallas kernels: 1.42 us -> 1.83 us  [body(): pl.pallas_call(functools.partial(finish, cell_halo_list.shape[1]), out_sh...]
where the time goes in v9:
time: 17.4 us; the launch traced here: 17.2 us
  Pallas kernels  16.6 us (95%)
  between operations  0.64 us (4%)
    pallas_call x1, Pallas kernels, body(): pl.pallas_call(functools.partial(kernel, lax.axis_size('mesh'), lax.axis_...  14.8 us
    pallas_call x1, Pallas kernels, body(): pl.pallas_call(functools.partial(finish, cell_halo_list.shape[1]), out_sh...  1.83 us

profile of v9, /device:TPU:0, one launch (start us, length us, event | category | flops | bytes accessed | tf_op | source)
XLA Modules:
  0.0 17.2 jit_solution(5882184924536901808)
XLA Ops:
  0.6 14.8 %shard_map.157 = (f32[2,3072]{1,0:T(2,128)}, f32[2,3072]{1,0:T(2,128)}, f32[2,1024]{1,0:T(2,128)}, f32[48,128]{1,0:T(8,128)}) custom-call(f32[2,3072]{1,0:T(2,128)} %vel_h.1, f32[2,3072]{1,0:T(2,128)} %thk_h.1, f32[2,3072]{1,0:T(2,128)} %vor_h.1, f32[2,3072]{1,0:T(2,128)} %wind_h.1, f32[10,3072]{1,0:T(8,128)} %wts_h.1, s32[10,3072]{1,0:T(8,128)} %eoe_h.1, ...), custom_call_target="tpu_custom_call" | custom-call | tf_op jit(solution)/shard_map/pallas_call | solution.py:457
  15.4 1.8 %shard_map.158 = (f32[2,3072]{1,0:T(2,128)}, f32[2,3072]{1,0:T(2,128)}, f32[2,1024]{1,0:T(2,128)}) custom-call(f32[48,128]{1,0:T(8,128)} %get-tuple-element.7.crecv_h, f32[2,1024]{1,0:T(2,128)} %get-tuple-element.8.energy_h, s32[2,3072]{1,0:T(2,128)} %coe_h.1, f32[24,128]{1,0:T(8,128)} %bitcast.1, f32[2,3072]{1,0:T(2,128)} %get-tuple-element.9.tend_h, ...), custom_call_target="tpu_custom_call" | custom-call | tf_op jit(solution)/shard_map/pallas_call | solution.py:482

commit v10 on v9

--- a/solution.py
+++ b/solution.py
@@ -244,21 +244,12 @@
             copy.wait()
         loads[7].wait()
 
-        for o in range(blocks):
-            for i in range(pairs_of):
-                first = SUB * o + levels + 2 * i
-                code_halo[SUB * o + i : SUB * o + i + 1, :] = coded(
-                    erecv[first : first + 1, :], erecv[first + 1 : first + 2, :]
-                )
-
         found = scan(edge_rows, edge_rows + blocks, halo_rows(range(levels), False), cell_lookups, found, blocks)
         for c in range(cell_rows):
             weight = padded_rows(ew[:, c * LANES : (c + 1) * LANES])
             energy[:, c * LANES : (c + 1) * LANES] = jnp.concatenate(
                 [total_rows(weight * found[c][l] * found[c][l]) for l in range(levels)], axis=0
             )
-
-        energy_out.start()
 
         for copy in loads[9:11]:
             copy.wait()
@@ -275,6 +266,13 @@
                 csend[SUB * o + l : SUB * o + l + 1, :] = block[o : o + 1]
         for copy in cell_copies:
             copy.start()
+        energy_out.start()
+        for o in range(blocks):
+            for i in range(pairs_of):
+                first = SUB * o + levels + 2 * i
+                code_halo[SUB * o + i : SUB * o + i + 1, :] = coded(
+                    erecv[first : first + 1, :], erecv[first + 1 : first + 2, :]
+                )
 
     def unit_step(u, carry):
         pl.when(u == units // 6)(edges_leave)

time: 17.4 us -> 17.4 us (level)
  no operation moved by 1% of the time
where the time goes in v10:
time: 17.4 us; the launch traced here: 17.2 us
  Pallas kernels  16.6 us (95%)
  between operations  0.64 us (4%)
    pallas_call x1, Pallas kernels, body(): pl.pallas_call(functools.partial(kernel, lax.axis_size('mesh'), lax.axis_...  14.7 us
    pallas_call x1, Pallas kernels, body(): pl.pallas_call(functools.partial(finish, cell_halo_list.shape[1]), out_sh...  1.83 us

profile of v10, /device:TPU:0, one launch (start us, length us, event | category | flops | bytes accessed | tf_op | source)
XLA Modules:
  0.0 17.2 jit_solution(15823781566386765025)
XLA Ops:
  0.6 14.7 %shard_map.157 = (f32[2,3072]{1,0:T(2,128)}, f32[2,3072]{1,0:T(2,128)}, f32[2,1024]{1,0:T(2,128)}, f32[48,128]{1,0:T(8,128)}) custom-call(f32[2,3072]{1,0:T(2,128)} %vel_h.1, f32[2,3072]{1,0:T(2,128)} %thk_h.1, f32[2,3072]{1,0:T(2,128)} %vor_h.1, f32[2,3072]{1,0:T(2,128)} %wind_h.1, f32[10,3072]{1,0:T(8,128)} %wts_h.1, s32[10,3072]{1,0:T(8,128)} %eoe_h.1, ...), custom_call_target="tpu_custom_call" | custom-call | tf_op jit(solution)/shard_map/pallas_call | solution.py:455
  15.4 1.8 %shard_map.158 = (f32[2,3072]{1,0:T(2,128)}, f32[2,3072]{1,0:T(2,128)}, f32[2,1024]{1,0:T(2,128)}) custom-call(f32[48,128]{1,0:T(8,128)} %get-tuple-element.7.crecv_h, f32[2,1024]{1,0:T(2,128)} %get-tuple-element.8.energy_h, s32[2,3072]{1,0:T(2,128)} %coe_h.1, f32[24,128]{1,0:T(8,128)} %bitcast.1, f32[2,3072]{1,0:T(2,128)} %get-tuple-element.9.tend_h, ...), custom_call_target="tpu_custom_call" | custom-call | tf_op jit(solution)/shard_map/pallas_call | solution.py:480
